TPU v7x, 32 devices: a whole 2x2x4 slice. The times are simulated.
32 devices in a mesh: grp: 4 (over x, core), dev: 8 (over z, y).
Axes of the slice: x: 2, y: 2, z: 4, core: 2. Of those that a mesh axis runs over, the one named last changes fastest.
Arguments:
- queries: bfloat16 [65536, 768], P(('grp', 'dev')), may hold values from -18 to 18
- passages: bfloat16 [8192, 768], P('dev'), may hold values from -5 to 5
- positives: int32 [512], P(('grp', 'dev')), may hold values from 0 to 63
- mined_blocks: int32 [512, 9], P(('grp', 'dev')), may hold values from 0 to 63, as said below
- counts: int32 [512], P(('grp', 'dev')), may hold values from 1 to 9, as said below
Outputs:
- losses: float32 [512, 128], P(('grp', 'dev'))
- query_grad: bfloat16 [65536, 768], P(('grp', 'dev'))
- passage_grad: float32 [8192, 768], P('dev')
Inputs may be any that keep to these rules, and one draw needn't show every extreme that they name: `mined_blocks`: the first counts[b] entries of row b are distinct and differ from positives[b]; later entries are ignored. Over the live entries and the positives of the 16 query blocks of one device, at most 2 distinct blocks have the same id // 8; in every draw some value of id // 8 has 2 distinct blocks on every device. `counts`: on every device some query block has 9.
All inputs are finite; a program needn't handle non-finite values.
Results may differ from a plain program's by a relative error of at most 0.0038.
Values may be sent and summed in bfloat16 or wider, within the bound.
A program may use at most 128 MiB of HBM per device.

v0:
```python
import math

import jax
import jax.numpy as jnp
from jax import lax
from jax.sharding import PartitionSpec as P

QROWS = 128
PROWS = 128
MAXL = 9
CAP = 2


def list_entries(positives, mined_blocks, counts):
    total_blocks = positives.shape[0]
    block_ids = jnp.concatenate([positives[:, None], mined_blocks], axis=1)
    tail_live = jnp.arange(MAXL, dtype=jnp.int32)[None, :] < counts[:, None]
    is_live = jnp.concatenate([jnp.ones((total_blocks, 1), dtype=jnp.bool_), tail_live], axis=1)
    return (block_ids, is_live)


def build_table(block_ids, is_live, shard_blocks, owners):
    flat_ids = block_ids.reshape(-1)
    flat_live = is_live.reshape(-1)
    entry_count = flat_ids.shape[0]
    position = jnp.arange(entry_count, dtype=jnp.int32)
    owner_of = flat_ids // shard_blocks
    local_id = flat_ids % shard_blocks
    matching = (flat_ids[:, None] == flat_ids[None, :]) & flat_live[:, None] & flat_live[None, :]
    earlier = position[None, :] < position[:, None]
    leading = flat_live & jnp.logical_not(jnp.any(matching & earlier, axis=1))
    leader = jnp.min(jnp.where(matching, position[None, :], entry_count), axis=1)
    leader = jnp.where(flat_live, leader, 0)
    same_owner = owner_of[:, None] == owner_of[None, :]
    standing = jnp.sum((leading[None, :] & same_owner & earlier).astype(jnp.int32), axis=1)
    place = standing[leader]
    slot_index = jnp.where(flat_live, owner_of * CAP + place, 0).reshape(block_ids.shape)
    owner_range = jnp.arange(owners, dtype=jnp.int32)
    place_range = jnp.arange(CAP, dtype=jnp.int32)
    chosen = (
        leading[:, None, None]
        & (owner_of[:, None, None] == owner_range[None, :, None])
        & (standing[:, None, None] == place_range[None, None, :])
    )
    request = jnp.sum(chosen.astype(jnp.int32) * local_id[:, None, None], axis=0)
    return (slot_index, request)


def padded_pass(query_blocks, fetched, slot_index, is_live, factor):
    slot_total = slot_index.shape[1]
    row_count = query_blocks.shape[1]
    col_count = fetched.shape[1]
    diagonal_mask = (jnp.arange(row_count)[:, None] == jnp.arange(col_count)[None, :]).astype(
        jnp.float32
    )
    target = jnp.where((jnp.arange(slot_total) == 0)[None, :, None], diagonal_mask[:, None, :], 0.0)

    def visit(grad_sum, inputs):
        query_rows, index_row, live_row = inputs
        candidates = fetched[index_row]
        scores = (
            jnp.einsum("qd,spd->qsp", query_rows, candidates, preferred_element_type=jnp.float32)
            * factor
        )
        scores = jnp.where(live_row[None, :, None], scores, -jnp.inf)
        largest = jnp.max(scores, axis=(1, 2), keepdims=True)
        log_total = largest + jnp.log(
            jnp.sum(jnp.exp(scores - largest), axis=(1, 2), keepdims=True)
        )
        row_losses = log_total[:, 0, 0] - jnp.diagonal(scores[:, 0, :])
        weights = (jnp.exp(scores - log_total) - target).astype(jnp.bfloat16)
        query_part = jnp.einsum(
            "qsp,spd->qd", weights, candidates, preferred_element_type=jnp.float32
        )
        passage_part = jnp.einsum(
            "qsp,qd->spd", weights, query_rows, preferred_element_type=jnp.float32
        )
        grad_sum = grad_sum.at[index_row].add(passage_part)
        return (grad_sum, (row_losses, query_part.astype(jnp.bfloat16)))

    start = jnp.zeros(fetched.shape, jnp.float32)
    return lax.scan(visit, start, (query_blocks, slot_index, is_live))


def body(queries, passages, positives, mined_blocks, counts):
    owners = lax.axis_size("dev")
    width = queries.shape[1]
    shard_blocks = passages.shape[0] // PROWS
    block_total = positives.shape[0]
    block_ids, is_live = list_entries(positives, mined_blocks, counts)
    slot_index, request = build_table(block_ids, is_live, shard_blocks, owners)
    wanted = lax.all_to_all(request, "dev", split_axis=0, concat_axis=0, tiled=True)
    blocks = passages.reshape(shard_blocks, PROWS, width)
    outgoing = blocks[wanted]
    fetched = lax.all_to_all(outgoing, "dev", split_axis=0, concat_axis=0, tiled=True).reshape(
        owners * CAP, PROWS, width
    )
    query_blocks = queries.reshape(block_total, QROWS, width)
    factor = 1.0 / math.sqrt(width)
    slot_grads, outputs = padded_pass(query_blocks, fetched, slot_index, is_live, factor)
    losses, query_grad = outputs
    returned = lax.all_to_all(
        slot_grads.reshape(owners, CAP, PROWS, width),
        "dev",
        split_axis=0,
        concat_axis=0,
        tiled=True,
    )
    shard_grad = jnp.zeros((shard_blocks, PROWS, width), jnp.float32)
    shard_grad = shard_grad.at[wanted.reshape(-1)].add(returned.reshape(owners * CAP, PROWS, width))
    passage_grad = lax.psum(shard_grad.reshape(shard_blocks * PROWS, width), "grp")
    return (losses, query_grad.reshape(block_total * QROWS, width), passage_grad)


def solution(mesh):
    return jax.shard_map(
        body,
        mesh=mesh,
        in_specs=(
            P(("grp", "dev"), None),
            P("dev", None),
            P(("grp", "dev")),
            P(("grp", "dev"), None),
            P(("grp", "dev")),
        ),
        out_specs=(P(("grp", "dev"), None), P(("grp", "dev"), None), P("dev", None)),
        check_vma=False,
    )
```

profile of v0, /device:TPU:0, one launch (start us, length us, event | category | flops | bytes accessed | tf_op | source)
XLA Modules:
  0.0 806.7 jit_solution(1310141557960999391)
XLA Ops:
  11.8 13.5 %all_to_all.22 = s32[8,1,2]{2,1,0:T(1,128)S(1)} all-to-all(s32[8,1,2]{2,1,0:T(1,128)S(1)} %copy.23), channel_id=1, replica_groups=mesh['grp'=4,'dev'=8] {'dev'}, dimensions={0} | all-to-all | bytes 128 | tf_op jit(solution)/shard_map/all_to_all | solution.py:92
  28.0 4.6 all-to-all-start.1
  36.6 65.5 %all-to-all-done.1 = bf16[8,2,128,768]{3,2,1,0:T(8,128)(2,1)} async-done(((bf16[8,2,128,768]{3,2,1,0:T(8,128)(2,1)}), bf16[8,2,128,768]{3,2,1,0:T(8,128)(2,1)}, u32[]{:S(2)}, u32[]{:S(2)}) %all-to-all-start.1) | async-done | bytes 3145760 | tf_op jit(solution)/shard_map/all_to_all | solution.py:95
  105.4 460.4 %while.15 = (s32[]{:T(128)}, f32[16,128,768]{2,1,0:T(8,128)}, f32[16,128]{1,0:T(8,128)}, bf16[16,128,768]{2,1,0:T(8,128)(2,1)}, s32[16,10]{1,0:T(8,128)}, /*inde...) while((s32[]{:T(128)}, f32[16,128,768]{2,1,0:T(8,128)}, ...), condition=%wide.region_8.9_spmd.clone, body=%wide.region_4.8_spmd.clone.sunk | while | flops 758187520 | bytes 29704628 | solution.py:82
  116.1 3.8 fusion.48
  120.0 10.4 %scatter_fusion = f32[16,128,768]{2,1,0:T(8,128)} fusion(f32[16,128,768]{2,1,0:T(8,128)} %get-tuple-element.187, s32[10]{0:T(128)S(1)} %fusion.46, f32[10,128,768]{2,1,0:T(8,128)} %fusion.48), kind=kCustom, calls=%fused_computation.4.clone.clone.1 | custom fusion | flops 983040 | bytes 11796520 | tf_op jit(solution)/shard_map/while/body/eval_jaxpr/scatter-add | solution.py:78
  144.8 3.8 fusion.48
  148.6 10.6 %scatter_fusion = f32[16,128,768]{2,1,0:T(8,128)} fusion(f32[16,128,768]{2,1,0:T(8,128)} %get-tuple-element.187, s32[10]{0:T(128)S(1)} %fusion.46, f32[10,128,768]{2,1,0:T(8,128)} %fusion.48), kind=kCustom, calls=%fused_computation.4.clone.clone.1 | custom fusion | flops 983040 | bytes 11796520 | tf_op jit(solution)/shard_map/while/body/eval_jaxpr/scatter-add | solution.py:78
  173.6 3.8 fusion.48
  177.4 10.4 %scatter_fusion = f32[16,128,768]{2,1,0:T(8,128)} fusion(f32[16,128,768]{2,1,0:T(8,128)} %get-tuple-element.187, s32[10]{0:T(128)S(1)} %fusion.46, f32[10,128,768]{2,1,0:T(8,128)} %fusion.48), kind=kCustom, calls=%fused_computation.4.clone.clone.1 | custom fusion | flops 983040 | bytes 11796520 | tf_op jit(solution)/shard_map/while/body/eval_jaxpr/scatter-add | solution.py:78
  206.1 10.6 %scatter_fusion = f32[16,128,768]{2,1,0:T(8,128)} fusion(f32[16,128,768]{2,1,0:T(8,128)} %get-tuple-element.187, s32[10]{0:T(128)S(1)} %fusion.46, f32[10,128,768]{2,1,0:T(8,128)} %fusion.48), kind=kCustom, calls=%fused_computation.4.clone.clone.1 | custom fusion | flops 983040 | bytes 11796520 | tf_op jit(solution)/shard_map/while/body/eval_jaxpr/scatter-add | solution.py:78
  231.0 3.8 fusion.48
  234.9 10.6 %scatter_fusion = f32[16,128,768]{2,1,0:T(8,128)} fusion(f32[16,128,768]{2,1,0:T(8,128)} %get-tuple-element.187, s32[10]{0:T(128)S(1)} %fusion.46, f32[10,128,768]{2,1,0:T(8,128)} %fusion.48), kind=kCustom, calls=%fused_computation.4.clone.clone.1 | custom fusion | flops 983040 | bytes 11796520 | tf_op jit(solution)/shard_map/while/body/eval_jaxpr/scatter-add | solution.py:78
  263.7 10.5 %scatter_fusion = f32[16,128,768]{2,1,0:T(8,128)} fusion(f32[16,128,768]{2,1,0:T(8,128)} %get-tuple-element.187, s32[10]{0:T(128)S(1)} %fusion.46, f32[10,128,768]{2,1,0:T(8,128)} %fusion.48), kind=kCustom, calls=%fused_computation.4.clone.clone.1 | custom fusion | flops 983040 | bytes 11796520 | tf_op jit(solution)/shard_map/while/body/eval_jaxpr/scatter-add | solution.py:78
  292.4 10.4 %scatter_fusion = f32[16,128,768]{2,1,0:T(8,128)} fusion(f32[16,128,768]{2,1,0:T(8,128)} %get-tuple-element.187, s32[10]{0:T(128)S(1)} %fusion.46, f32[10,128,768]{2,1,0:T(8,128)} %fusion.48), kind=kCustom, calls=%fused_computation.4.clone.clone.1 | custom fusion | flops 983040 | bytes 11796520 | tf_op jit(solution)/shard_map/while/body/eval_jaxpr/scatter-add | solution.py:78
  321.1 10.3 %scatter_fusion = f32[16,128,768]{2,1,0:T(8,128)} fusion(f32[16,128,768]{2,1,0:T(8,128)} %get-tuple-element.187, s32[10]{0:T(128)S(1)} %fusion.46, f32[10,128,768]{2,1,0:T(8,128)} %fusion.48), kind=kCustom, calls=%fused_computation.4.clone.clone.1 | custom fusion | flops 983040 | bytes 11796520 | tf_op jit(solution)/shard_map/while/body/eval_jaxpr/scatter-add | solution.py:78
  349.6 11.0 %scatter_fusion = f32[16,128,768]{2,1,0:T(8,128)} fusion(f32[16,128,768]{2,1,0:T(8,128)} %get-tuple-element.187, s32[10]{0:T(128)S(1)} %fusion.46, f32[10,128,768]{2,1,0:T(8,128)} %fusion.48), kind=kCustom, calls=%fused_computation.4.clone.clone.1 | custom fusion | flops 983040 | bytes 11796520 | tf_op jit(solution)/shard_map/while/body/eval_jaxpr/scatter-add | solution.py:78
  378.9 10.5 %scatter_fusion = f32[16,128,768]{2,1,0:T(8,128)} fusion(f32[16,128,768]{2,1,0:T(8,128)} %get-tuple-element.187, s32[10]{0:T(128)S(1)} %fusion.46, f32[10,128,768]{2,1,0:T(8,128)} %fusion.48), kind=kCustom, calls=%fused_computation.4.clone.clone.1 | custom fusion | flops 983040 | bytes 11796520 | tf_op jit(solution)/shard_map/while/body/eval_jaxpr/scatter-add | solution.py:78
  403.9 3.8 fusion.48
  407.7 10.4 %scatter_fusion = f32[16,128,768]{2,1,0:T(8,128)} fusion(f32[16,128,768]{2,1,0:T(8,128)} %get-tuple-element.187, s32[10]{0:T(128)S(1)} %fusion.46, f32[10,128,768]{2,1,0:T(8,128)} %fusion.48), kind=kCustom, calls=%fused_computation.4.clone.clone.1 | custom fusion | flops 983040 | bytes 11796520 | tf_op jit(solution)/shard_map/while/body/eval_jaxpr/scatter-add | solution.py:78
  432.6 3.8 fusion.48
  436.4 10.6 %scatter_fusion = f32[16,128,768]{2,1,0:T(8,128)} fusion(f32[16,128,768]{2,1,0:T(8,128)} %get-tuple-element.187, s32[10]{0:T(128)S(1)} %fusion.46, f32[10,128,768]{2,1,0:T(8,128)} %fusion.48), kind=kCustom, calls=%fused_computation.4.clone.clone.1 | custom fusion | flops 983040 | bytes 11796520 | tf_op jit(solution)/shard_map/while/body/eval_jaxpr/scatter-add | solution.py:78
  465.2 10.4 %scatter_fusion = f32[16,128,768]{2,1,0:T(8,128)} fusion(f32[16,128,768]{2,1,0:T(8,128)} %get-tuple-element.187, s32[10]{0:T(128)S(1)} %fusion.46, f32[10,128,768]{2,1,0:T(8,128)} %fusion.48), kind=kCustom, calls=%fused_computation.4.clone.clone.1 | custom fusion | flops 983040 | bytes 11796520 | tf_op jit(solution)/shard_map/while/body/eval_jaxpr/scatter-add | solution.py:78
  493.9 10.5 %scatter_fusion = f32[16,128,768]{2,1,0:T(8,128)} fusion(f32[16,128,768]{2,1,0:T(8,128)} %get-tuple-element.187, s32[10]{0:T(128)S(1)} %fusion.46, f32[10,128,768]{2,1,0:T(8,128)} %fusion.48), kind=kCustom, calls=%fused_computation.4.clone.clone.1 | custom fusion | flops 983040 | bytes 11796520 | tf_op jit(solution)/shard_map/while/body/eval_jaxpr/scatter-add | solution.py:78
  518.9 3.8 fusion.48
  522.7 10.6 %scatter_fusion = f32[16,128,768]{2,1,0:T(8,128)} fusion(f32[16,128,768]{2,1,0:T(8,128)} %get-tuple-element.187, s32[10]{0:T(128)S(1)} %fusion.46, f32[10,128,768]{2,1,0:T(8,128)} %fusion.48), kind=kCustom, calls=%fused_computation.4.clone.clone.1 | custom fusion | flops 983040 | bytes 11796520 | tf_op jit(solution)/shard_map/while/body/eval_jaxpr/scatter-add | solution.py:78
  547.8 3.8 fusion.48
  551.6 10.6 %scatter_fusion = f32[16,128,768]{2,1,0:T(8,128)} fusion(f32[16,128,768]{2,1,0:T(8,128)} %get-tuple-element.187, s32[10]{0:T(128)S(1)} %fusion.46, f32[10,128,768]{2,1,0:T(8,128)} %fusion.48), kind=kCustom, calls=%fused_computation.4.clone.clone.1 | custom fusion | flops 983040 | bytes 11796520 | tf_op jit(solution)/shard_map/while/body/eval_jaxpr/scatter-add | solution.py:78
  565.9 9.1 %all-to-all-start.2 = ((f32[8,2,128,768]{3,2,1,0:T(8,128)}), f32[8,2,128,768]{3,2,1,0:T(8,128)}, u32[]{:S(2)}, u32[]{:S(2)}) async-start(f32[8,2,128,768]{3,2,1,0:T(8,128)} %bitcast.81), calls=%async_computation.2 | async-start | bytes 12582912 | tf_op jit(solution)/shard_map/all_to_all | solution.py:102
  576.2 131.3 %all-to-all-done.2 = f32[8,2,128,768]{3,2,1,0:T(8,128)} async-done(((f32[8,2,128,768]{3,2,1,0:T(8,128)}), f32[8,2,128,768]{3,2,1,0:T(8,128)}, u32[]{:S(2)}, u32[]{:S(2)}) %all-to-all-start.2) | async-done | bytes 6291488 | tf_op jit(solution)/shard_map/all_to_all | solution.py:102
  709.5 15.0 %scatter_fusion.1 = f32[8,128,768]{2,1,0:T(8,128)} fusion(f32[8,128,768]{2,1,0:T(8,128)} %broadcast_in_dim.106, s32[16]{0:T(128)S(1)} %fusion.28, f32[16,128,768]{2,1,0:T(8,128)} %bitcast.12), kind=kCustom, calls=%fused_computation.5 | custom fusion | flops 1572864 | bytes 18874432 | tf_op jit(solution)/shard_map/scatter-add | solution.py:110
  724.5 71.6 %all-reduce.3.cloned.1.call-done = f32[1024,768]{1,0:T(8,128)} async-done(((f32[1024,768]{1,0:T(8,128)}), f32[1024,768]{1,0:T(8,128)}) %all-reduce.3.cloned.1.call-update) | async-done | bytes 3145744 | tf_op jit(solution)/shard_map/psum | solution.py:111
  (312 shorter events, 282.4 us)
Async XLA Ops:
  7.2 18.4 %copy-start = (bf16[1024,768]{1,0:T(8,128)(2,1)S(1)}, bf16[1024,768]{1,0:T(8,128)(2,1)}, u32[]{:S(2)}) copy-start(bf16[1024,768]{1,0:T(8,128)(2,1)} %param.8) | copy-start | bytes 4718596
  25.3 2.7 copy-start.3
  28.0 7.9 copy-start.5
  28.0 74.1 %all-to-all-start.1 = ((bf16[8,2,128,768]{3,2,1,0:T(8,128)(2,1)}), bf16[8,2,128,768]{3,2,1,0:T(8,128)(2,1)}, u32[]{:S(2)}, u32[]{:S(2)}) async-start(bf16[8,2,128,768]{3,2,1,0:T(8,128)(2,1)} %bitcast.83), calls=%async_computation.1 | async-start | bytes 6291456 | tf_op jit(solution)/shard_map/all_to_all | solution.py:95
  111.0 0.8 copy-start.1
  120.0 12.8 %copy-start.2 = (f32[1,128]{1,0:T(1,128)S(1)}, f32[1,128]{1,0:T(1,128)}, u32[]{:S(2)}) copy-start(f32[1,128]{1,0:T(1,128)} %get-tuple-element.173) | copy-start | bytes 1540 | tf_op jit(solution)/shard_map/while
  139.6 0.8 copy-start.1
  148.6 13.0 %copy-start.2 = (f32[1,128]{1,0:T(1,128)S(1)}, f32[1,128]{1,0:T(1,128)}, u32[]{:S(2)}) copy-start(f32[1,128]{1,0:T(1,128)} %get-tuple-element.173) | copy-start | bytes 1540 | tf_op jit(solution)/shard_map/while
  168.4 0.8 copy-start.1
  177.4 12.8 %copy-start.2 = (f32[1,128]{1,0:T(1,128)S(1)}, f32[1,128]{1,0:T(1,128)}, u32[]{:S(2)}) copy-start(f32[1,128]{1,0:T(1,128)} %get-tuple-element.173) | copy-start | bytes 1540 | tf_op jit(solution)/shard_map/while
  197.0 0.8 copy-start.1
  206.1 13.0 %copy-start.2 = (f32[1,128]{1,0:T(1,128)S(1)}, f32[1,128]{1,0:T(1,128)}, u32[]{:S(2)}) copy-start(f32[1,128]{1,0:T(1,128)} %get-tuple-element.173) | copy-start | bytes 1540 | tf_op jit(solution)/shard_map/while
  225.8 0.8 copy-start.1
  234.9 13.0 %copy-start.2 = (f32[1,128]{1,0:T(1,128)S(1)}, f32[1,128]{1,0:T(1,128)}, u32[]{:S(2)}) copy-start(f32[1,128]{1,0:T(1,128)} %get-tuple-element.173) | copy-start | bytes 1540 | tf_op jit(solution)/shard_map/while
  254.7 0.8 copy-start.1
  263.7 13.0 %copy-start.2 = (f32[1,128]{1,0:T(1,128)S(1)}, f32[1,128]{1,0:T(1,128)}, u32[]{:S(2)}) copy-start(f32[1,128]{1,0:T(1,128)} %get-tuple-element.173) | copy-start | bytes 1540 | tf_op jit(solution)/shard_map/while
  283.4 0.8 copy-start.1
  292.4 12.8 %copy-start.2 = (f32[1,128]{1,0:T(1,128)S(1)}, f32[1,128]{1,0:T(1,128)}, u32[]{:S(2)}) copy-start(f32[1,128]{1,0:T(1,128)} %get-tuple-element.173) | copy-start | bytes 1540 | tf_op jit(solution)/shard_map/while
  321.1 12.7 %copy-start.2 = (f32[1,128]{1,0:T(1,128)S(1)}, f32[1,128]{1,0:T(1,128)}, u32[]{:S(2)}) copy-start(f32[1,128]{1,0:T(1,128)} %get-tuple-element.173) | copy-start | bytes 1540 | tf_op jit(solution)/shard_map/while
  349.6 13.5 %copy-start.2 = (f32[1,128]{1,0:T(1,128)S(1)}, f32[1,128]{1,0:T(1,128)}, u32[]{:S(2)}) copy-start(f32[1,128]{1,0:T(1,128)} %get-tuple-element.173) | copy-start | bytes 1540 | tf_op jit(solution)/shard_map/while
  378.9 12.9 %copy-start.2 = (f32[1,128]{1,0:T(1,128)S(1)}, f32[1,128]{1,0:T(1,128)}, u32[]{:S(2)}) copy-start(f32[1,128]{1,0:T(1,128)} %get-tuple-element.173) | copy-start | bytes 1540 | tf_op jit(solution)/shard_map/while
  407.7 12.9 %copy-start.2 = (f32[1,128]{1,0:T(1,128)S(1)}, f32[1,128]{1,0:T(1,128)}, u32[]{:S(2)}) copy-start(f32[1,128]{1,0:T(1,128)} %get-tuple-element.173) | copy-start | bytes 1540 | tf_op jit(solution)/shard_map/while
  427.4 0.8 copy-start.1
  436.4 13.0 %copy-start.2 = (f32[1,128]{1,0:T(1,128)S(1)}, f32[1,128]{1,0:T(1,128)}, u32[]{:S(2)}) copy-start(f32[1,128]{1,0:T(1,128)} %get-tuple-element.173) | copy-start | bytes 1540 | tf_op jit(solution)/shard_map/while
  465.2 12.8 %copy-start.2 = (f32[1,128]{1,0:T(1,128)S(1)}, f32[1,128]{1,0:T(1,128)}, u32[]{:S(2)}) copy-start(f32[1,128]{1,0:T(1,128)} %get-tuple-element.173) | copy-start | bytes 1540 | tf_op jit(solution)/shard_map/while
  484.9 0.8 copy-start.1
  493.9 13.0 %copy-start.2 = (f32[1,128]{1,0:T(1,128)S(1)}, f32[1,128]{1,0:T(1,128)}, u32[]{:S(2)}) copy-start(f32[1,128]{1,0:T(1,128)} %get-tuple-element.173) | copy-start | bytes 1540 | tf_op jit(solution)/shard_map/while
  522.7 13.0 %copy-start.2 = (f32[1,128]{1,0:T(1,128)S(1)}, f32[1,128]{1,0:T(1,128)}, u32[]{:S(2)}) copy-start(f32[1,128]{1,0:T(1,128)} %get-tuple-element.173) | copy-start | bytes 1540 | tf_op jit(solution)/shard_map/while
  551.6 13.0 %copy-start.2 = (f32[1,128]{1,0:T(1,128)S(1)}, f32[1,128]{1,0:T(1,128)}, u32[]{:S(2)}) copy-start(f32[1,128]{1,0:T(1,128)} %get-tuple-element.173) | copy-start | bytes 1540 | tf_op jit(solution)/shard_map/while
  565.9 9.6 %copy-start.4 = (s32[8,1,2]{2,1,0:T(1,128)S(1)}, s32[8,1,2]{2,1,0:T(1,128)}, u32[]{:S(2)}) copy-start(s32[8,1,2]{2,1,0:T(1,128)} %copy-done.3) | copy-start | bytes 196
  565.9 141.7 %all-to-all-start.2 = ((f32[8,2,128,768]{3,2,1,0:T(8,128)}), f32[8,2,128,768]{3,2,1,0:T(8,128)}, u32[]{:S(2)}, u32[]{:S(2)}) async-start(f32[8,2,128,768]{3,2,1,0:T(8,128)} %bitcast.81), calls=%async_computation.2 | async-start | bytes 12582912 | tf_op jit(solution)/shard_map/all_to_all | solution.py:102
  574.9 221.2 %all-reduce.3.cloned.1.call-start = ((), (), s32[]{:S(2)}) async-start(), calls=%async_computation.3 | async-start | bytes 6291456 | tf_op jit(solution)/shard_map/psum | solution.py:111
  (7 other events, 5.9 us)
Sparse Core Ops, SparseCore 0:
  724.7 71.4 all-reduce.2
where the time goes:
time: 812 us; the launch traced here: 807 us
  waiting for transfers between devices  268 us (33%)
  other arithmetic  230 us (28%)
  local copies, waits for them, and re-layouts  142 us (17%)
  matrix products  125 us (15%)
  between operations  14.2 us (2%)
  starting transfers between devices  13.7 us (2%)
  blocking collectives  13.5 us (2%)
    scatter-add x16, other arithmetic, visit(): grad_sum = grad_sum.at[index_row].add(passage_part)  169 us
    all_to_all x1, waiting for transfers between devices, body(): lax.all_to_all(slot_grads.reshape(owners, CAP, PROWS, width), 'dev', spli...  131 us
    psum x1, waiting for transfers between devices, body(): lax.psum(shard_grad.reshape(shard_blocks * PROWS, width), 'grp')  71.6 us
    all_to_all x1, waiting for transfers between devices, body(): lax.all_to_all(outgoing, 'dev', split_axis=0, concat_axis=0, tiled=True)  65.5 us
    dot_general x16, matrix products, visit(): jnp.einsum('qsp,qd->spd', weights, query_rows, preferred_element_type=jnp...  61.2 us
    gather x16, local copies, waits for them, and re-layouts, visit(): candidates = fetched[index_row]  41 us
    gather x16, local copies, waits for them, and re-layouts, visit(): row_losses = log_total[:, 0, 0] - jnp.diagonal(scores[:, 0, :])  40.4 us
    dot_general x16, matrix products, visit(): jnp.einsum('qsp,spd->qd', weights, candidates, preferred_element_type=jnp...  38.4 us
  transfers between devices with their start and end apart: 3, of which 3 were waited for; matrix products, arithmetic and copies ran while one was open for 1% of the time, Pallas kernels for 0%

commit v1 on v0

--- a/solution.py
+++ b/solution.py
@@ -46,40 +46,28 @@
     return (slot_index, request)
 
 
-def padded_pass(query_blocks, fetched, slot_index, is_live, factor):
-    slot_total = slot_index.shape[1]
-    row_count = query_blocks.shape[1]
-    col_count = fetched.shape[1]
-    diagonal_mask = (jnp.arange(row_count)[:, None] == jnp.arange(col_count)[None, :]).astype(
-        jnp.float32
-    )
-    target = jnp.where((jnp.arange(slot_total) == 0)[None, :, None], diagonal_mask[:, None, :], 0.0)
-
-    def visit(grad_sum, inputs):
-        query_rows, index_row, live_row = inputs
-        candidates = fetched[index_row]
-        scores = (
-            jnp.einsum("qd,spd->qsp", query_rows, candidates, preferred_element_type=jnp.float32)
-            * factor
-        )
-        scores = jnp.where(live_row[None, :, None], scores, -jnp.inf)
-        largest = jnp.max(scores, axis=(1, 2), keepdims=True)
-        log_total = largest + jnp.log(
-            jnp.sum(jnp.exp(scores - largest), axis=(1, 2), keepdims=True)
-        )
-        row_losses = log_total[:, 0, 0] - jnp.diagonal(scores[:, 0, :])
-        weights = (jnp.exp(scores - log_total) - target).astype(jnp.bfloat16)
-        query_part = jnp.einsum(
-            "qsp,spd->qd", weights, candidates, preferred_element_type=jnp.float32
-        )
-        passage_part = jnp.einsum(
-            "qsp,qd->spd", weights, query_rows, preferred_element_type=jnp.float32
-        )
-        grad_sum = grad_sum.at[index_row].add(passage_part)
-        return (grad_sum, (row_losses, query_part.astype(jnp.bfloat16)))
-
-    start = jnp.zeros(fetched.shape, jnp.float32)
-    return lax.scan(visit, start, (query_blocks, slot_index, is_live))
+def dense_pass(queries, fetched, slot_index, is_live, factor):
+    block_total = slot_index.shape[0]
+    slots = fetched.shape[0]
+    width = queries.shape[1]
+    flat = fetched.reshape(slots * PROWS, width)
+    slot_range = jnp.arange(slots, dtype=jnp.int32)
+    used = jnp.any((slot_index[:, :, None] == slot_range) & is_live[:, :, None], axis=1)
+    positive = (slot_index[:, 0, None] == slot_range).astype(jnp.float32)
+    scores = jnp.einsum("qd,pd->qp", queries, flat, preferred_element_type=jnp.float32) * factor
+    scores = scores.reshape(block_total, QROWS, slots, PROWS)
+    scores = jnp.where(used[:, None, :, None], scores, -jnp.inf)
+    diagonal = jnp.eye(QROWS, PROWS, dtype=jnp.float32)
+    target = positive[:, None, :, None] * diagonal[None, :, None, :]
+    largest = jnp.max(scores, axis=(2, 3), keepdims=True)
+    log_total = largest + jnp.log(jnp.sum(jnp.exp(scores - largest), axis=(2, 3), keepdims=True))
+    hit = jnp.sum(jnp.where(target > 0, scores, 0.0), axis=(2, 3))
+    losses = log_total[:, :, 0, 0] - hit
+    weights = (jnp.exp(scores - log_total) - target).astype(jnp.bfloat16)
+    weights = weights.reshape(block_total * QROWS, slots * PROWS)
+    query_grad = jnp.einsum("qp,pd->qd", weights, flat, preferred_element_type=jnp.float32)
+    slot_grads = jnp.einsum("qp,qd->pd", weights, queries, preferred_element_type=jnp.float32)
+    return slot_grads.astype(jnp.bfloat16), (losses, query_grad.astype(jnp.bfloat16))
 
 
 def body(queries, passages, positives, mined_blocks, counts):
@@ -95,9 +83,8 @@
     fetched = lax.all_to_all(outgoing, "dev", split_axis=0, concat_axis=0, tiled=True).reshape(
         owners * CAP, PROWS, width
     )
-    query_blocks = queries.reshape(block_total, QROWS, width)
     factor = 1.0 / math.sqrt(width)
-    slot_grads, outputs = padded_pass(query_blocks, fetched, slot_index, is_live, factor)
+    slot_grads, outputs = dense_pass(queries, fetched, slot_index, is_live, factor)
     losses, query_grad = outputs
     returned = lax.all_to_all(
         slot_grads.reshape(owners, CAP, PROWS, width),
@@ -106,8 +93,13 @@
         concat_axis=0,
         tiled=True,
     )
-    shard_grad = jnp.zeros((shard_blocks, PROWS, width), jnp.float32)
-    shard_grad = shard_grad.at[wanted.reshape(-1)].add(returned.reshape(owners * CAP, PROWS, width))
+    place = (jnp.arange(shard_blocks, dtype=jnp.int32)[:, None] == wanted.reshape(-1)).astype(jnp.bfloat16)
+    shard_grad = jnp.einsum(
+        "bs,sd->bd",
+        place,
+        returned.reshape(owners * CAP, PROWS * width),
+        preferred_element_type=jnp.float32,
+    )
     passage_grad = lax.psum(shard_grad.reshape(shard_blocks * PROWS, width), "grp")
     return (losses, query_grad.reshape(block_total * QROWS, width), passage_grad)
 

time: 812 us -> 321 us (0.40)
  other arithmetic: 230 us -> 38.9 us
  local copies, waits for them, and re-layouts: 142 us -> 22.2 us
  matrix products: 125 us -> 37.9 us
  waiting for transfers between devices: 268 us -> 185 us
    scatter-add x17 -> x0, other arithmetic: 184 us -> none  [the longest x16 169 us: visit(): grad_sum = grad_sum.at[index_row].add(passage_part)]
    dot_general x48 -> x4, matrix products: 125 us -> 37.9 us  [the longest x1 13.8 us: dense_pass(): jnp.einsum('qd,pd->qp', queries, flat, preferred_element_type=jnp.float32)]
    gather x32 -> x0, local copies, waits for them, and re-layouts: 81.4 us -> none  [the longest x16 41 us: visit(): candidates = fetched[index_row]]
    all_to_all x1, waiting for transfers between devices: 131 us -> 69.5 us  [body(): lax.all_to_all(slot_grads.reshape(owners, CAP, PROWS, width), 'dev', spli...]
    dynamic_update_slice x16 -> x0, local copies, waits for them, and re-layouts: 20.6 us -> none  [padded_pass(): return lax.scan(visit, start, (query_blocks, slot_index, is_live))]
    sub x16 -> x1, other arithmetic: 19 us -> 0.61 us  [dense_pass(): losses = log_total[:, :, 0, 0] - hit]
    psum x1, waiting for transfers between devices: 71.6 us -> 55.9 us  [body(): lax.psum(shard_grad.reshape(shard_blocks * PROWS, width), 'grp')]
    broadcast_in_dim x18 -> x1, local copies, waits for them, and re-layouts: 15.8 us -> 1.15 us  [dense_pass(): scores = jnp.where(used[:, None, :, None], scores, -jnp.inf)]
  transfers between devices with their start and end apart: 3 -> 3, of which waited for: 3 -> 3; matrix products, arithmetic and copies ran while one was open for 1% -> 7% of each run, Pallas kernels for 0% -> 0%
where the time goes in v1:
time: 321 us; the launch traced here: 320 us
  waiting for transfers between devices  185 us (58%)
  other arithmetic  38.9 us (12%)
  matrix products  37.9 us (12%)
  local copies, waits for them, and re-layouts  22.2 us (7%)
  between operations  14.2 us (4%)
  blocking collectives  13.5 us (4%)
  starting transfers between devices  8.27 us (3%)
    all_to_all x1, waiting for transfers between devices, body(): lax.all_to_all(slot_grads.reshape(owners, CAP, PROWS, width), 'dev', spli...  69.5 us
    all_to_all x1, waiting for transfers between devices, body(): lax.all_to_all(outgoing, 'dev', split_axis=0, concat_axis=0, tiled=True)  59.5 us
    psum x1, waiting for transfers between devices, body(): lax.psum(shard_grad.reshape(shard_blocks * PROWS, width), 'grp')  55.9 us
    convert_element_type x1, other arithmetic, dense_pass(): weights = (jnp.exp(scores - log_total) - target).astype(jnp.bfloat16)  14.8 us
    dot_general x1, matrix products, dense_pass(): jnp.einsum('qd,pd->qp', queries, flat, preferred_element_type=jnp.float32)  13.8 us
    all_to_all x1, blocking collectives, body(): lax.all_to_all(request, 'dev', split_axis=0, concat_axis=0, tiled=True)  13.5 us
    reduce_sum x1, other arithmetic, dense_pass(): hit = jnp.sum(jnp.where(target > 0, scores, 0.0), axis=(2, 3))  12.8 us
    dot_general x1, matrix products, dense_pass(): jnp.einsum('qp,pd->qd', weights, flat, preferred_element_type=jnp.float32)  11.7 us
  transfers between devices with their start and end apart: 3, of which 3 were waited for; matrix products, arithmetic and copies ran while one was open for 7% of the time, Pallas kernels for 0%

profile of v1, /device:TPU:0, one launch (start us, length us, event | category | flops | bytes accessed | tf_op | source)
XLA Modules:
  0.0 320.1 jit_solution(6734878062235327881)
XLA Ops:
  7.2 0.9 iota_compare_fusion.5
  8.2 0.7 copy.18
  9.0 0.8 pad_add_fusion
  9.9 0.2 fusion.3
  10.1 0.2 convert_reduce_fusion
  10.3 0.1 select_reduce_fusion.2
  10.5 13.5 %all_to_all.22 = s32[8,1,2]{2,1,0:T(1,128)S(1)} all-to-all(s32[8,1,2]{2,1,0:T(1,128)S(1)} %copy.22), channel_id=1, replica_groups=mesh['grp'=4,'dev'=8] {'dev'}, dimensions={0} | all-to-all | bytes 128 | tf_op jit(solution)/shard_map/all_to_all | solution.py:80
  24.3 3.8 %gather_fusion.1 = bf16[16,128,768]{2,1,0:T(8,128)(2,1)} fusion(bf16[8,128,768]{2,1,0:T(8,128)(2,1)} %bitcast.50, s32[1024]{0:T(1024)S(1)} %pad_clamp_fusion), kind=kCustom, calls=%fused_computation.1 | custom fusion | bytes 6291520 | tf_op jit(solution)/shard_map/gather | solution.py:82
  28.2 4.6 %all-to-all-start.1 = ((bf16[8,2,128,768]{3,2,1,0:T(8,128)(2,1)}), bf16[8,2,128,768]{3,2,1,0:T(8,128)(2,1)}, u32[]{:S(2)}, u32[]{:S(2)}) async-start(bf16[8,2,128,768]{3,2,1,0:T(8,128)(2,1)} %bitcast.49), calls=%async_computation.1 | async-start | bytes 6291456 | tf_op jit(solution)/shard_map/all_to_all | solution.py:83
  33.0 0.2 select_reduce_fusion.1
  33.2 1.6 gather_fusion
  35.1 0.1 fusion.5
  35.3 0.1 slice_reduce_fusion
  35.4 7.4 %broadcast_multiply_fusion = f32[16,128,16,128]{1,0,3,2:T(8,128)} fusion(f32[128,128]{0,1:T(8,128)S(1)} %fusion.6, f32[16,16]{0,1:T(8,128)S(1)} %fusion.13), kind=kLoop, calls=%fused_computation.8 | loop fusion | flops 4194304 | bytes 16843776 | tf_op jit(solution)/shard_map/mul | solution.py:61
  42.8 59.5 %all-to-all-done.1 = bf16[8,2,128,768]{3,2,1,0:T(8,128)(2,1)} async-done(((bf16[8,2,128,768]{3,2,1,0:T(8,128)(2,1)}), bf16[8,2,128,768]{3,2,1,0:T(8,128)(2,1)}, u32[]{:S(2)}, u32[]{:S(2)}) %all-to-all-start.1) | async-done | bytes 3145760 | tf_op jit(solution)/shard_map/all_to_all | solution.py:83
  102.3 1.1 broadcast_in_dim.28
  103.5 13.8 %fusion.16 = (f32[2048]{0:T(1024)S(1)}, f32[2048,2048]{0,1:T(8,128)}) fusion(bf16[2048,768]{1,0:T(8,128)(2,1)} %bitcast.7, bf16[2048,768]{1,0:T(8,128)(2,1)S(1)} %copy-done, pred[256,8,16,128]{3,2,1,0:T(8,128)(4,1)S(1)} %bitcast.51), kind=kOutput, calls=%fused_computation.59 | convolution fusion | flops 6455031808 | bytes 27271168 | tf_op jit(solution)/shard_map/qd,pd->qp/dot_general | solution.py:57
  117.4 12.8 %select_reduce_fusion = (f32[2048]{0:T(1024)S(1)}, f32[2048]{0:T(1024)S(1)}) fusion(f32[2048,2048]{0,1:T(8,128)} %get-tuple-element.10, f32[256,8,16,128]{3,2,1,0:T(8,128)S(1)} %bitcast.45, f32[2048]{0:T(1024)S(1)} %get-tuple-element.9), kind=kLoop, calls=%fused_computation.6 | loop fusion | flops 20967424 | bytes 33579008 | tf_op jit(solution)/shard_map/reduce_sum | solution.py:64
  130.1 0.6 subtract_bitcast_fusion
  130.8 14.8 %fusion = bf16[2048,2048]{0,1:T(8,128)(2,1)} fusion(f32[2048,2048]{0,1:T(8,128)} %get-tuple-element.10, f32[256,8,16,128]{3,2,1,0:T(8,128)S(1)} %bitcast.46, f32[2048]{0:T(1024)S(1)} %get-tuple-element.6), kind=kLoop, calls=%fused_computation.4 | loop fusion | flops 12582912 | bytes 41951232 | tf_op jit(solution)/shard_map/convert_element_type | solution.py:66
  145.5 10.2 %convolution_convert_fusion = bf16[2048,768]{1,0:T(8,128)(2,1)} fusion(bf16[2048,2048]{0,1:T(8,128)(2,1)} %fusion, bf16[2048,768]{1,0:T(8,128)(2,1)S(1)} %copy-done), kind=kOutput, calls=%fused_computation.9 | convolution fusion | flops 6444023808 | bytes 14680064 | tf_op jit(solution)/shard_map/qp,qd->pd/dot_general | solution.py:69
  155.7 3.7 %all-to-all-start.2 = ((bf16[8,2,128,768]{3,2,1,0:T(8,128)(2,1)}), bf16[8,2,128,768]{3,2,1,0:T(8,128)(2,1)S(1)}, u32[]{:S(2)}, u32[]{:S(2)}) async-start(bf16[8,2,128,768]{3,2,1,0:T(8,128)(2,1)} %bitcast.52), calls=%async_computation.2 | async-start | bytes 6291456 | tf_op jit(solution)/shard_map/all_to_all | solution.py:89
  159.4 0.5 broadcast.305
  159.9 0.7 reduce.8
  160.7 69.5 %all-to-all-done.2 = bf16[8,2,128,768]{3,2,1,0:T(8,128)(2,1)S(1)} async-done(((bf16[8,2,128,768]{3,2,1,0:T(8,128)(2,1)}), bf16[8,2,128,768]{3,2,1,0:T(8,128)(2,1)S(1)}, u32[]{:S(2)}, u32[]{:S(2)}) %all-to-all-start.2) | async-done | bytes 3145760 | tf_op jit(solution)/shard_map/all_to_all | solution.py:89
  230.2 1.7 copy-done.2
  231.9 3.6 %copy.27 = bf16[2,8,128,768]{3,1,2,0:T(8,128)(2,1)S(1)} copy(bf16[2,8,128,768]{3,2,1,0:T(8,128)(2,1)} %bitcast.48) | data formatting | bytes 6291456
  235.5 2.2 fusion.14
  237.7 4.1 %reshape.365 = f32[1024,768]{1,0:T(8,128)} reshape(f32[8,98304]{1,0:T(8,128)} %fusion.14) | data formatting | bytes 6291456 | tf_op jit(solution)/shard_map/reshape | solution.py:103
  241.9 11.7 %convolution_convert_fusion.1 = bf16[2048,768]{1,0:T(8,128)(2,1)} fusion(bf16[2048,2048]{0,1:T(8,128)(2,1)} %fusion, bf16[2048,768]{1,0:T(8,128)(2,1)} %bitcast.7), kind=kOutput, calls=%fused_computation.10 | convolution fusion | flops 6444023808 | bytes 14680064 | tf_op jit(solution)/shard_map/qp,pd->qd/dot_general | solution.py:68
  253.6 55.9 %all-reduce.3.cloned.1.call-done = f32[1024,768]{1,0:T(8,128)} async-done(((f32[1024,768]{1,0:T(8,128)}), f32[1024,768]{1,0:T(8,128)}) %all-reduce.3.cloned.1.call-update) | async-done | bytes 3145744 | tf_op jit(solution)/shard_map/psum | solution.py:103
  309.5 3.8 %copy.32 = f32[1024,768]{1,0:T(8,128)} copy(f32[1024,768]{1,0:T(8,128)} %all-reduce.3.cloned.1.call-done) | data formatting | bytes 6291456
  (42 shorter events, 1.4 us)
Async XLA Ops:
  7.2 96.3 %copy-start = (bf16[2048,768]{1,0:T(8,128)(2,1)S(1)}, bf16[2048,768]{1,0:T(8,128)(2,1)}, u32[]{:S(2)}) copy-start(bf16[2048,768]{1,0:T(8,128)(2,1)} %param.5) | copy-start | bytes 9437188
  28.2 6.7 %copy-start.3 = (s32[16,9]{1,0:T(8,128)S(1)}, s32[16,9]{1,0:T(8,128)}, u32[]{:S(2)}) copy-start(s32[16,9]{1,0:T(8,128)} %param.8) | copy-start | bytes 1732
  28.2 74.1 %all-to-all-start.1 = ((bf16[8,2,128,768]{3,2,1,0:T(8,128)(2,1)}), bf16[8,2,128,768]{3,2,1,0:T(8,128)(2,1)}, u32[]{:S(2)}, u32[]{:S(2)}) async-start(bf16[8,2,128,768]{3,2,1,0:T(8,128)(2,1)} %bitcast.49), calls=%async_computation.1 | async-start | bytes 6291456 | tf_op jit(solution)/shard_map/all_to_all | solution.py:83
  103.5 13.9 %slice-start = ((s8[16777216]{0:T(1024)(128)(4,1)}), s8[4194304]{0:T(1024)(128)(4,1)S(1)}, s32[]{:S(2)}) async-start(s8[16777216]{0:T(1024)(128)(4,1)} %bitcast.43), calls=%async_computation.4 | async-start | bytes 8388608
  103.5 13.9 %slice-start.1 = ((s8[16777216]{0:T(1024)(128)(4,1)}), s8[4194304]{0:T(1024)(128)(4,1)S(1)}, s32[]{:S(2)}) async-start(s8[16777216]{0:T(1024)(128)(4,1)} %bitcast.43), calls=%async_computation.5 | async-start | bytes 8388608
  103.5 13.9 %slice-start.2 = ((s8[16777216]{0:T(1024)(128)(4,1)}), s8[4194304]{0:T(1024)(128)(4,1)S(1)}, s32[]{:S(2)}) async-start(s8[16777216]{0:T(1024)(128)(4,1)} %bitcast.43), calls=%async_computation.6 | async-start | bytes 8388608
  103.5 13.9 %slice-start.3 = ((s8[16777216]{0:T(1024)(128)(4,1)}), s8[4194304]{0:T(1024)(128)(4,1)S(1)}, s32[]{:S(2)}) async-start(s8[16777216]{0:T(1024)(128)(4,1)} %bitcast.43), calls=%async_computation.7 | async-start | bytes 8388608
  155.7 74.5 %all-to-all-start.2 = ((bf16[8,2,128,768]{3,2,1,0:T(8,128)(2,1)}), bf16[8,2,128,768]{3,2,1,0:T(8,128)(2,1)S(1)}, u32[]{:S(2)}, u32[]{:S(2)}) async-start(bf16[8,2,128,768]{3,2,1,0:T(8,128)(2,1)} %bitcast.52), calls=%async_computation.2 | async-start | bytes 6291456 | tf_op jit(solution)/shard_map/all_to_all | solution.py:89
  159.4 150.2 %all-reduce.3.cloned.1.call-start = ((), (), s32[]{:S(2)}) async-start(), calls=%async_computation.3 | async-start | bytes 6291456 | tf_op jit(solution)/shard_map/psum | solution.py:103
  230.2 1.7 copy-start.2
  241.8 71.4 %copy-start.1 = (bf16[2048,768]{1,0:T(8,128)(2,1)S(1)}, bf16[2048,768]{1,0:T(8,128)(2,1)}, u32[]{:S(2)}) copy-start(bf16[2048,768]{1,0:T(8,128)(2,1)} %param.5) | copy-start | bytes 9437188
Sparse Core Ops, SparseCore 0:
  242.0 67.4 all-reduce.2

commit v2 on v1

--- a/solution.py
+++ b/solution.py
@@ -72,35 +72,50 @@
 
 def body(queries, passages, positives, mined_blocks, counts):
     owners = lax.axis_size("dev")
+    groups = lax.axis_size("grp")
     width = queries.shape[1]
     shard_blocks = passages.shape[0] // PROWS
     block_total = positives.shape[0]
     block_ids, is_live = list_entries(positives, mined_blocks, counts)
     slot_index, request = build_table(block_ids, is_live, shard_blocks, owners)
-    wanted = lax.all_to_all(request, "dev", split_axis=0, concat_axis=0, tiled=True)
+    requests = lax.all_gather(request, ("grp", "dev"), axis=0, tiled=False)
+    asked = lax.dynamic_index_in_dim(requests, lax.axis_index("dev"), axis=1, keepdims=False)
+    wanted = lax.dynamic_slice_in_dim(asked, lax.axis_index("grp") * owners, owners, axis=0)
     blocks = passages.reshape(shard_blocks, PROWS, width)
-    outgoing = blocks[wanted]
+    outgoing = jnp.concatenate(
+        [
+            lax.dynamic_slice_in_dim(blocks, wanted[source, place], 1, axis=0)
+            for source in range(owners)
+            for place in range(CAP)
+        ],
+        axis=0,
+    ).reshape(owners, CAP, PROWS, width)
     fetched = lax.all_to_all(outgoing, "dev", split_axis=0, concat_axis=0, tiled=True).reshape(
         owners * CAP, PROWS, width
     )
     factor = 1.0 / math.sqrt(width)
     slot_grads, outputs = dense_pass(queries, fetched, slot_index, is_live, factor)
     losses, query_grad = outputs
+    part = PROWS // groups
+    sending = slot_grads.reshape(owners, CAP, groups, part, width).transpose(2, 0, 1, 3, 4)
     returned = lax.all_to_all(
-        slot_grads.reshape(owners, CAP, PROWS, width),
-        "dev",
+        sending.reshape(groups * owners, CAP, part, width),
+        ("grp", "dev"),
         split_axis=0,
         concat_axis=0,
         tiled=True,
     )
-    place = (jnp.arange(shard_blocks, dtype=jnp.int32)[:, None] == wanted.reshape(-1)).astype(jnp.bfloat16)
-    shard_grad = jnp.einsum(
+    place = (jnp.arange(shard_blocks, dtype=jnp.int32)[:, None] == asked.reshape(-1)).astype(jnp.bfloat16)
+    share = jnp.einsum(
         "bs,sd->bd",
         place,
-        returned.reshape(owners * CAP, PROWS * width),
+        returned.reshape(groups * owners * CAP, part * width),
         preferred_element_type=jnp.float32,
     )
-    passage_grad = lax.psum(shard_grad.reshape(shard_blocks * PROWS, width), "grp")
+    share = share.astype(jnp.bfloat16).reshape(shard_blocks, part, width)
+    gathered = lax.all_gather(share, "grp", axis=0, tiled=False)
+    passage_grad = gathered.transpose(1, 0, 2, 3).reshape(shard_blocks * PROWS, width)
+    passage_grad = passage_grad.astype(jnp.float32)
     return (losses, query_grad.reshape(block_total * QROWS, width), passage_grad)
 
 

time: 321 us -> 355 us (1.11)
  blocking collectives: 13.5 us -> 69.7 us
  waiting for transfers between devices: 185 us -> 135 us
  between operations: 14.2 us -> 44.5 us
    all_gather x0 -> x1, blocking collectives: none -> 69.7 us  [body(): requests = lax.all_gather(request, ('grp', 'dev'), axis=0, tiled=False)]
    psum x1 -> x0, waiting for transfers between devices: 55.9 us -> none  [body(): lax.psum(shard_grad.reshape(shard_blocks * PROWS, width), 'grp')]
    all_to_all x1 -> x0, blocking collectives: 13.5 us -> none  [body(): lax.all_to_all(request, 'dev', split_axis=0, concat_axis=0, tiled=True)]
    all_gather x0 -> x1, waiting for transfers between devices: none -> 5.81 us  [body(): gathered = lax.all_gather(share, 'grp', axis=0, tiled=False)]
    gather x1 -> x0, local copies, waits for them, and re-layouts: 3.82 us -> none  [body(): outgoing = blocks[wanted]]
    unnamed x18 -> x34, local copies, waits for them, and re-layouts: 9.09 us -> 11.4 us
  transfers between devices with their start and end apart: 3 -> 3, of which waited for: 3 -> 3; matrix products, arithmetic and copies ran while one was open for 7% -> 6% of each run, Pallas kernels for 0% -> 0%
where the time goes in v2:
time: 355 us; the launch traced here: 354 us
  waiting for transfers between devices  135 us (38%)
  blocking collectives  69.7 us (20%)
  between operations  44.5 us (13%)
  other arithmetic  41.7 us (12%)
  matrix products  35.1 us (10%)
  local copies, waits for them, and re-layouts  20.2 us (6%)
  starting transfers between devices  8.02 us (2%)
    all_to_all x1, waiting for transfers between devices, body(): lax.all_to_all(sending.reshape(groups * owners, CAP, part, width), ('grp'...  72.2 us
    all_gather x1, blocking collectives, body(): requests = lax.all_gather(request, ('grp', 'dev'), axis=0, tiled=False)  69.7 us
    all_to_all x1, waiting for transfers between devices, body(): lax.all_to_all(outgoing, 'dev', split_axis=0, concat_axis=0, tiled=True)  56.9 us
    convert_element_type x1, other arithmetic, dense_pass(): weights = (jnp.exp(scores - log_total) - target).astype(jnp.bfloat16)  14.8 us
    dot_general x1, matrix products, dense_pass(): jnp.einsum('qd,pd->qp', queries, flat, preferred_element_type=jnp.float32)  13.8 us
    reduce_sum x1, other arithmetic, dense_pass(): hit = jnp.sum(jnp.where(target > 0, scores, 0.0), axis=(2, 3))  12.8 us
    dot_general x1, matrix products, dense_pass(): jnp.einsum('qp,pd->qd', weights, flat, preferred_element_type=jnp.float32)  11.7 us
    unnamed x34, local copies, waits for them, and re-layouts  11.4 us
  transfers between devices with their start and end apart: 3, of which 3 were waited for; matrix products, arithmetic and copies ran while one was open for 6% of the time, Pallas kernels for 0%

profile of v2, /device:TPU:0, one launch (start us, length us, event | category | flops | bytes accessed | tf_op | source)
XLA Modules:
  0.0 354.2 jit_solution(7060164537876135144)
XLA Ops:
  7.2 0.9 iota_compare_fusion.5
  8.2 0.7 copy.24
  9.0 0.8 pad_add_fusion
  10.5 69.7 %all-gather.1 = s32[32,8,2]{1,2,0:T(2,128)S(1)} all-gather(s32[1,8,2]{1,2,0:T(2,128)S(1)} %bitcast.92), channel_id=2, replica_groups=mesh['grp'=4,'dev'=8] {'grp','dev'}, dimensions={0}, use_global_device_ids=true | all-gather | bytes 2112 | tf_op jit(solution)/shard_map/all_gather | solution.py:81
  80.4 0.7 fusion.15
  111.3 1.1 dynamic-slice_dynamic-update-slice_fusion.15
  112.3 0.9 dynamic-slice_dynamic-update-slice_fusion.14
  113.3 0.9 dynamic-slice_dynamic-update-slice_fusion.13
  114.2 0.9 dynamic-slice_dynamic-update-slice_fusion.12
  115.2 0.9 dynamic-slice_dynamic-update-slice_fusion.11
  116.1 0.9 dynamic-slice_dynamic-update-slice_fusion.10
  117.1 0.9 dynamic-slice_dynamic-update-slice_fusion.9
  118.0 0.9 dynamic-slice_dynamic-update-slice_fusion.8
  119.2 1.7 copy-done.3
  120.9 4.6 %all-to-all-start = ((bf16[8,2,128,768]{3,2,1,0:T(8,128)(2,1)}), bf16[8,2,128,768]{3,2,1,0:T(8,128)(2,1)}, u32[]{:S(2)}, u32[]{:S(2)}) async-start(bf16[8,2,128,768]{3,2,1,0:T(8,128)(2,1)} %bitcast.87), calls=%async_computation | async-start | bytes 6291456 | tf_op jit(solution)/shard_map/all_to_all | solution.py:93
  125.9 1.6 gather_fusion
  128.1 7.4 %broadcast_multiply_fusion = f32[16,128,16,128]{1,0,3,2:T(8,128)} fusion(f32[128,128]{0,1:T(8,128)S(1)} %fusion.6, f32[16,16]{0,1:T(8,128)S(1)} %fusion.13), kind=kLoop, calls=%fused_computation.8 | loop fusion | flops 4194304 | bytes 16843776 | tf_op jit(solution)/shard_map/mul | solution.py:61
  135.5 56.9 %all-to-all-done = bf16[8,2,128,768]{3,2,1,0:T(8,128)(2,1)} async-done(((bf16[8,2,128,768]{3,2,1,0:T(8,128)(2,1)}), bf16[8,2,128,768]{3,2,1,0:T(8,128)(2,1)}, u32[]{:S(2)}, u32[]{:S(2)}) %all-to-all-start) | async-done | bytes 3145760 | tf_op jit(solution)/shard_map/all_to_all | solution.py:93
  192.4 1.1 broadcast_in_dim.28
  193.6 13.8 %fusion.16 = (f32[2048]{0:T(1024)S(1)}, f32[2048,2048]{0,1:T(8,128)}) fusion(bf16[2048,768]{1,0:T(8,128)(2,1)} %bitcast.23, bf16[2048,768]{1,0:T(8,128)(2,1)S(1)} %copy-done, pred[256,8,16,128]{3,2,1,0:T(8,128)(4,1)S(1)} %bitcast.86), kind=kOutput, calls=%fused_computation.76 | convolution fusion | flops 6455031808 | bytes 27271168 | tf_op jit(solution)/shard_map/qd,pd->qp/dot_general | solution.py:57
  207.5 12.8 %select_reduce_fusion = (f32[2048]{0:T(1024)S(1)}, f32[2048]{0:T(1024)S(1)}) fusion(f32[2048,2048]{0,1:T(8,128)} %get-tuple-element.26, f32[256,8,16,128]{3,2,1,0:T(8,128)S(1)} %bitcast.65, f32[2048]{0:T(1024)S(1)} %get-tuple-element.25), kind=kLoop, calls=%fused_computation.6 | loop fusion | flops 20967424 | bytes 33579008 | tf_op jit(solution)/shard_map/reduce_sum | solution.py:64
  220.9 14.8 %fusion = bf16[2048,2048]{0,1:T(8,128)(2,1)} fusion(f32[2048,2048]{0,1:T(8,128)} %get-tuple-element.26, f32[256,8,16,128]{3,2,1,0:T(8,128)S(1)} %bitcast.66, f32[2048]{0:T(1024)S(1)} %get-tuple-element.6), kind=kLoop, calls=%fused_computation.4 | loop fusion | flops 12582912 | bytes 41951232 | tf_op jit(solution)/shard_map/convert_element_type | solution.py:66
  235.7 9.0 %convolution_convert_fusion.1 = bf16[2048,768]{1,0:T(8,128)(2,1)S(1)} fusion(bf16[2048,2048]{0,1:T(8,128)(2,1)} %fusion, bf16[2048,768]{1,0:T(8,128)(2,1)S(1)} %copy-done), kind=kOutput, calls=%fused_computation.9 | convolution fusion | flops 6444023808 | bytes 14680064 | tf_op jit(solution)/shard_map/qp,qd->pd/dot_general | solution.py:69
  244.7 1.9 copy.29
  246.7 3.4 all-to-all-start.1
  250.1 0.7 dynamic-slice_reduce_fusion
  250.9 72.2 %all-to-all-done.1 = bf16[32,2,32,768]{3,2,1,0:T(8,128)(2,1)S(1)} async-done(((bf16[32,2,32,768]{3,2,1,0:T(8,128)(2,1)}), bf16[32,2,32,768]{3,2,1,0:T(8,128)(2,1)S(1)}, u32[]{:S(2)}, u32[]{:S(2)}) %all-to-all-start.1) | async-done | bytes 3145760 | tf_op jit(solution)/shard_map/all_to_all | solution.py:101
  323.1 1.8 copy.34
  325.5 0.8 copy.30
  326.4 11.7 %convolution_convert_fusion.2 = bf16[2048,768]{1,0:T(8,128)(2,1)} fusion(bf16[2048,2048]{0,1:T(8,128)(2,1)} %fusion, bf16[2048,768]{1,0:T(8,128)(2,1)} %bitcast.23), kind=kOutput, calls=%fused_computation.10 | convolution fusion | flops 6444023808 | bytes 14680064 | tf_op jit(solution)/shard_map/qp,pd->qd/dot_general | solution.py:68
  338.1 5.8 %all-gather.4.cloned.1.call-done = bf16[4,8,32,768]{3,2,1,0:T(8,128)(2,1)} async-done(((bf16[1,8,32,768]{3,2,1,0:T(8,128)(2,1)}), bf16[4,8,32,768]{3,2,1,0:T(8,128)(2,1)}) %all-gather.4.cloned.1.call-update) | async-done | bytes 1572880 | tf_op jit(solution)/shard_map/all_gather | solution.py:116
  343.9 3.5 copy_convert_fusion
  (56 shorter events, 3.5 us)
Async XLA Ops:
  7.2 186.4 %copy-start = (bf16[2048,768]{1,0:T(8,128)(2,1)S(1)}, bf16[2048,768]{1,0:T(8,128)(2,1)}, u32[]{:S(2)}) copy-start(bf16[2048,768]{1,0:T(8,128)(2,1)} %param.5) | copy-start | bytes 9437188
  111.2 7.7 %copy-start.2 = (bf16[1024,768]{1,0:T(8,128)(2,1)S(1)}, bf16[1024,768]{1,0:T(8,128)(2,1)}, u32[]{:S(2)}) copy-start(bf16[1024,768]{1,0:T(8,128)(2,1)} %param.6) | copy-start | bytes 4718596
  119.2 1.7 copy-start.3
  120.9 6.7 %copy-start.4 = (s32[16,9]{1,0:T(8,128)S(1)}, s32[16,9]{1,0:T(8,128)}, u32[]{:S(2)}) copy-start(s32[16,9]{1,0:T(8,128)} %param.8) | copy-start | bytes 1732
  120.9 71.5 %all-to-all-start = ((bf16[8,2,128,768]{3,2,1,0:T(8,128)(2,1)}), bf16[8,2,128,768]{3,2,1,0:T(8,128)(2,1)}, u32[]{:S(2)}, u32[]{:S(2)}) async-start(bf16[8,2,128,768]{3,2,1,0:T(8,128)(2,1)} %bitcast.87), calls=%async_computation | async-start | bytes 6291456 | tf_op jit(solution)/shard_map/all_to_all | solution.py:93
  193.6 13.9 %slice-start = ((s8[16777216]{0:T(1024)(128)(4,1)}), s8[4194304]{0:T(1024)(128)(4,1)S(1)}, s32[]{:S(2)}) async-start(s8[16777216]{0:T(1024)(128)(4,1)} %bitcast.63), calls=%async_computation.3 | async-start | bytes 8388608
  193.6 13.9 %slice-start.1 = ((s8[16777216]{0:T(1024)(128)(4,1)}), s8[4194304]{0:T(1024)(128)(4,1)S(1)}, s32[]{:S(2)}) async-start(s8[16777216]{0:T(1024)(128)(4,1)} %bitcast.63), calls=%async_computation.4 | async-start | bytes 8388608
  193.6 13.9 %slice-start.2 = ((s8[16777216]{0:T(1024)(128)(4,1)}), s8[4194304]{0:T(1024)(128)(4,1)S(1)}, s32[]{:S(2)}) async-start(s8[16777216]{0:T(1024)(128)(4,1)} %bitcast.63), calls=%async_computation.5 | async-start | bytes 8388608
  193.6 13.9 %slice-start.3 = ((s8[16777216]{0:T(1024)(128)(4,1)}), s8[4194304]{0:T(1024)(128)(4,1)S(1)}, s32[]{:S(2)}) async-start(s8[16777216]{0:T(1024)(128)(4,1)} %bitcast.63), calls=%async_computation.6 | async-start | bytes 8388608
  246.7 76.5 %all-to-all-start.1 = ((bf16[32,2,32,768]{3,2,1,0:T(8,128)(2,1)}), bf16[32,2,32,768]{3,2,1,0:T(8,128)(2,1)S(1)}, u32[]{:S(2)}, u32[]{:S(2)}) async-start(bf16[32,2,32,768]{3,2,1,0:T(8,128)(2,1)} %bitcast.68), calls=%async_computation.1 | async-start | bytes 6291456 | tf_op jit(solution)/shard_map/all_to_all | solution.py:101
  250.1 93.8 %all-gather.4.cloned.1.call-start = ((), (), s32[]{:S(2)}) async-start(), calls=%async_computation.2 | async-start | bytes 1966080 | tf_op jit(solution)/shard_map/all_gather | solution.py:116
  326.4 21.0 %copy-start.1 = (bf16[2048,768]{1,0:T(8,128)(2,1)S(1)}, bf16[2048,768]{1,0:T(8,128)(2,1)}, u32[]{:S(2)}) copy-start(bf16[2048,768]{1,0:T(8,128)(2,1)} %param.5) | copy-start | bytes 9437188
Sparse Core Ops, SparseCore 0:
  326.5 17.3 all-gather.3

commit v3 on v2

--- a/solution.py
+++ b/solution.py
@@ -78,18 +78,14 @@
     block_total = positives.shape[0]
     block_ids, is_live = list_entries(positives, mined_blocks, counts)
     slot_index, request = build_table(block_ids, is_live, shard_blocks, owners)
-    requests = lax.all_gather(request, ("grp", "dev"), axis=0, tiled=False)
-    asked = lax.dynamic_index_in_dim(requests, lax.axis_index("dev"), axis=1, keepdims=False)
-    wanted = lax.dynamic_slice_in_dim(asked, lax.axis_index("grp") * owners, owners, axis=0)
+    wanted = lax.all_to_all(request, "dev", split_axis=0, concat_axis=0, tiled=True)
+    asked = lax.all_gather(wanted, "grp", axis=0, tiled=False)
     blocks = passages.reshape(shard_blocks, PROWS, width)
-    outgoing = jnp.concatenate(
-        [
-            lax.dynamic_slice_in_dim(blocks, wanted[source, place], 1, axis=0)
-            for source in range(owners)
-            for place in range(CAP)
-        ],
-        axis=0,
-    ).reshape(owners, CAP, PROWS, width)
+    picks = wanted.reshape(-1)[:, None, None]
+    outgoing = jnp.broadcast_to(blocks[0][None], (owners * CAP, PROWS, width))
+    for local in range(1, shard_blocks):
+        outgoing = jnp.where(picks == local, blocks[local][None], outgoing)
+    outgoing = outgoing.reshape(owners, CAP, PROWS, width)
     fetched = lax.all_to_all(outgoing, "dev", split_axis=0, concat_axis=0, tiled=True).reshape(
         owners * CAP, PROWS, width
     )

time: 355 us -> 278 us (0.78)
  blocking collectives: 69.7 us -> 19.6 us
  between operations: 44.5 us -> 14.3 us
  waiting for transfers between devices: 135 us -> 121 us
  starting transfers between devices: 8.02 us -> 15.4 us
  other arithmetic: 41.7 us -> 48 us
    all_gather x1, blocking collectives: 69.7 us -> 19.6 us  [body(): asked = lax.all_gather(wanted, 'grp', axis=0, tiled=False)]
    all_to_all x1, waiting for transfers between devices: 72.2 us -> 52.1 us  [body(): lax.all_to_all(sending.reshape(groups * owners, CAP, part, width), ('grp'...]
    eq x0 -> x7, local copies, waits for them, and re-layouts: none -> 9.08 us  [body(): outgoing = jnp.where(picks == local, blocks[local][None], outgoing)]
    unnamed x34 -> x31, local copies, waits for them, and re-layouts: 11.4 us -> 2.84 us
    all_to_all x0 -> x1, starting transfers between devices: none -> 7.28 us  [body(): lax.all_to_all(request, 'dev', split_axis=0, concat_axis=0, tiled=True)]
    select_n x0 -> x1, other arithmetic: none -> 4.39 us  [body(): outgoing = jnp.where(picks == local, blocks[local][None], outgoing)]
    all_to_all x0 -> x1, waiting for transfers between devices: none -> 3.92 us  [body(): lax.all_to_all(request, 'dev', split_axis=0, concat_axis=0, tiled=True)]
  transfers between devices with their start and end apart: 3 -> 4, of which waited for: 3 -> 4; matrix products, arithmetic and copies ran while one was open for 6% -> 9% of each run, Pallas kernels for 0% -> 0%
where the time goes in v3:
time: 278 us; the launch traced here: 277 us
  waiting for transfers between devices  121 us (44%)
  other arithmetic  48 us (17%)
  matrix products  35.2 us (13%)
  local copies, waits for them, and re-layouts  23.4 us (8%)
  blocking collectives  19.6 us (7%)
  starting transfers between devices  15.4 us (6%)
  between operations  14.3 us (5%)
    all_to_all x1, waiting for transfers between devices, body(): lax.all_to_all(outgoing, 'dev', split_axis=0, concat_axis=0, tiled=True)  59.5 us
    all_to_all x1, waiting for transfers between devices, body(): lax.all_to_all(sending.reshape(groups * owners, CAP, part, width), ('grp'...  52.1 us
    all_gather x1, blocking collectives, body(): asked = lax.all_gather(wanted, 'grp', axis=0, tiled=False)  19.6 us
    convert_element_type x1, other arithmetic, dense_pass(): weights = (jnp.exp(scores - log_total) - target).astype(jnp.bfloat16)  14.8 us
    dot_general x1, matrix products, dense_pass(): jnp.einsum('qd,pd->qp', queries, flat, preferred_element_type=jnp.float32)  14 us
    reduce_sum x1, other arithmetic, dense_pass(): hit = jnp.sum(jnp.where(target > 0, scores, 0.0), axis=(2, 3))  12.8 us
    dot_general x1, matrix products, dense_pass(): jnp.einsum('qp,pd->qd', weights, flat, preferred_element_type=jnp.float32)  11.7 us
    eq x7, local copies, waits for them, and re-layouts, body(): outgoing = jnp.where(picks == local, blocks[local][None], outgoing)  9.08 us
  transfers between devices with their start and end apart: 4, of which 4 were waited for; matrix products, arithmetic and copies ran while one was open for 9% of the time, Pallas kernels for 0%

profile of v3, /device:TPU:0, one launch (start us, length us, event | category | flops | bytes accessed | tf_op | source)
XLA Modules:
  0.0 277.4 jit_solution(6229671455241050397)
XLA Ops:
  7.2 0.9 iota_compare_fusion.5
  9.6 0.8 pad_add_fusion
  12.1 7.3 %all-to-all-start = ((s32[8,1,2]{2,1,0:T(1,128)}), s32[8,1,2]{2,1,0:T(1,128)S(1)}, u32[]{:S(2)}, u32[]{:S(2)}) async-start(s32[8,1,2]{2,1,0:T(1,128)} %copy.92), calls=%async_computation | async-start | bytes 8192 | tf_op jit(solution)/shard_map/all_to_all | solution.py:81
  19.3 2.5 fusion.15
  21.8 3.9 %all-to-all-done = s32[8,1,2]{2,1,0:T(1,128)S(1)} async-done(((s32[8,1,2]{2,1,0:T(1,128)}), s32[8,1,2]{2,1,0:T(1,128)S(1)}, u32[]{:S(2)}, u32[]{:S(2)}) %all-to-all-start) | async-done | bytes 96 | tf_op jit(solution)/shard_map/all_to_all | solution.py:81
  26.4 1.3 compare_bitcast_fusion.6
  27.7 1.3 copy.94
  29.0 1.3 copy.106
  30.3 1.3 copy.104
  31.6 1.3 copy.102
  32.9 1.3 copy.100
  34.2 1.3 copy.98
  35.5 1.3 copy.96
  36.7 4.4 %select_select_fusion = bf16[8,2,128,768]{3,2,1,0:T(8,128)(2,1)} fusion(pred[8,2]{1,0:T(8,128)(4,1)} %copy.106, pred[8,2]{1,0:T(8,128)(4,1)} %copy.104, pred[8,2]{1,0:T(8,128)(4,1)} %copy.102, pred[8,2]{1,0:T(8,128)(4,1)} %copy.100, pred[8,2]{1,0:T(8,128)(4,1)} %copy.98, pred[8,2]{1,0:T(8,128)(4,1)} %copy.96, pred[8,2]{1,0:T(8,128)(4,1)} %copy.94, ...), kind=kLoop, calls=%fused_computation.11 | loop fusion | flops 11010048 | bytes 4718704 | tf_op jit(solution)/shard_map/jit(_where)/select_n | solution.py:87
  41.2 4.5 %all-to-all-start.1 = ((bf16[8,2,128,768]{3,2,1,0:T(8,128)(2,1)}), bf16[8,2,128,768]{3,2,1,0:T(8,128)(2,1)}, u32[]{:S(2)}, u32[]{:S(2)}) async-start(bf16[8,2,128,768]{3,2,1,0:T(8,128)(2,1)} %select_select_fusion), calls=%async_computation.1 | async-start | bytes 6291456 | tf_op jit(solution)/shard_map/all_to_all | solution.py:89
  46.1 1.6 gather_fusion
  48.4 7.4 %broadcast_multiply_fusion = f32[16,128,16,128]{1,0,3,2:T(8,128)} fusion(f32[128,128]{0,1:T(8,128)S(1)} %fusion.6, f32[16,16]{0,1:T(8,128)S(1)} %fusion.13), kind=kLoop, calls=%fused_computation.8 | loop fusion | flops 4194304 | bytes 16843776 | tf_op jit(solution)/shard_map/mul | solution.py:61
  55.7 59.5 %all-to-all-done.1 = bf16[8,2,128,768]{3,2,1,0:T(8,128)(2,1)} async-done(((bf16[8,2,128,768]{3,2,1,0:T(8,128)(2,1)}), bf16[8,2,128,768]{3,2,1,0:T(8,128)(2,1)}, u32[]{:S(2)}, u32[]{:S(2)}) %all-to-all-start.1) | async-done | bytes 3145760 | tf_op jit(solution)/shard_map/all_to_all | solution.py:89
  115.2 1.1 broadcast_in_dim.139
  116.4 14.0 %fusion.16 = (f32[2048]{0:T(1024)S(1)}, f32[2048,2048]{0,1:T(8,128)}) fusion(bf16[2048,768]{1,0:T(8,128)(2,1)} %bitcast.11, bf16[2048,768]{1,0:T(8,128)(2,1)S(1)} %copy-done, pred[256,8,16,128]{3,2,1,0:T(8,128)(4,1)S(1)} %bitcast.65), kind=kOutput, calls=%fused_computation.66 | convolution fusion | flops 6455031808 | bytes 27271168 | tf_op jit(solution)/shard_map/qd,pd->qp/dot_general | solution.py:57
  130.4 12.8 %select_reduce_fusion = (f32[2048]{0:T(1024)S(1)}, f32[2048]{0:T(1024)S(1)}) fusion(f32[2048,2048]{0,1:T(8,128)} %get-tuple-element.25, f32[256,8,16,128]{3,2,1,0:T(8,128)S(1)} %bitcast.60, f32[2048]{0:T(1024)S(1)} %get-tuple-element.24), kind=kLoop, calls=%fused_computation.6 | loop fusion | flops 20967424 | bytes 33579008 | tf_op jit(solution)/shard_map/reduce_sum | solution.py:64
  143.8 14.8 %fusion = bf16[2048,2048]{0,1:T(8,128)(2,1)} fusion(f32[2048,2048]{0,1:T(8,128)} %get-tuple-element.25, f32[256,8,16,128]{3,2,1,0:T(8,128)S(1)} %bitcast.61, f32[2048]{0:T(1024)S(1)} %get-tuple-element.6), kind=kLoop, calls=%fused_computation.4 | loop fusion | flops 12582912 | bytes 41951232 | tf_op jit(solution)/shard_map/convert_element_type | solution.py:66
  158.6 9.0 %convolution_convert_fusion.1 = bf16[2048,768]{1,0:T(8,128)(2,1)S(1)} fusion(bf16[2048,2048]{0,1:T(8,128)(2,1)} %fusion, bf16[2048,768]{1,0:T(8,128)(2,1)S(1)} %copy-done), kind=kOutput, calls=%fused_computation.9 | convolution fusion | flops 6444023808 | bytes 14680064 | tf_op jit(solution)/shard_map/qp,qd->pd/dot_general | solution.py:69
  167.6 1.9 copy.107
  169.6 3.6 %all-to-all-start.2 = ((bf16[32,2,32,768]{3,2,1,0:T(8,128)(2,1)}), bf16[32,2,32,768]{3,2,1,0:T(8,128)(2,1)S(1)}, u32[]{:S(2)}, u32[]{:S(2)}) async-start(bf16[32,2,32,768]{3,2,1,0:T(8,128)(2,1)} %bitcast.63), calls=%async_computation.2 | async-start | bytes 6291456 | tf_op jit(solution)/shard_map/all_to_all | solution.py:97
  173.3 19.6 %all-gather = s32[32,1,2]{2,1,0:T(1,128)S(1)} all-gather(s32[8,1,2]{2,1,0:T(1,128)S(1)} %all-to-all-done), channel_id=2, replica_groups=mesh['grp'=4,'dev'=8] {'grp'}, dimensions={0}, use_global_device_ids=true | all-gather | bytes 320 | tf_op jit(solution)/shard_map/all_gather | solution.py:82
  194.2 52.1 %all-to-all-done.2 = bf16[32,2,32,768]{3,2,1,0:T(8,128)(2,1)S(1)} async-done(((bf16[32,2,32,768]{3,2,1,0:T(8,128)(2,1)}), bf16[32,2,32,768]{3,2,1,0:T(8,128)(2,1)S(1)}, u32[]{:S(2)}, u32[]{:S(2)}) %all-to-all-start.2) | async-done | bytes 3145760 | tf_op jit(solution)/shard_map/all_to_all | solution.py:97
  246.3 1.8 copy.112
  248.7 0.8 copy.108
  249.5 11.7 %convolution_convert_fusion.2 = bf16[2048,768]{1,0:T(8,128)(2,1)} fusion(bf16[2048,2048]{0,1:T(8,128)(2,1)} %fusion, bf16[2048,768]{1,0:T(8,128)(2,1)} %bitcast.11), kind=kOutput, calls=%fused_computation.10 | convolution fusion | flops 6444023808 | bytes 14680064 | tf_op jit(solution)/shard_map/qp,pd->qd/dot_general | solution.py:68
  261.3 5.8 %all-gather.3.cloned.1.call-done = bf16[4,8,32,768]{3,2,1,0:T(8,128)(2,1)} async-done(((bf16[1,8,32,768]{3,2,1,0:T(8,128)(2,1)}), bf16[4,8,32,768]{3,2,1,0:T(8,128)(2,1)}) %all-gather.3.cloned.1.call-update) | async-done | bytes 1572880 | tf_op jit(solution)/shard_map/all_gather | solution.py:112
  267.1 3.5 %copy_convert_fusion = f32[4,8,32,768]{3,2,0,1:T(8,128)} fusion(bf16[4,8,32,768]{3,2,1,0:T(8,128)(2,1)} %all-gather.3.cloned.1.call-done), kind=kLoop, calls=%fused_computation.12 | loop fusion | flops 786432 | bytes 4718592 | tf_op jit(solution)/shard_map/convert_element_type | solution.py:114
  (64 shorter events, 7.3 us)
Async XLA Ops:
  7.2 109.2 %copy-start = (bf16[2048,768]{1,0:T(8,128)(2,1)S(1)}, bf16[2048,768]{1,0:T(8,128)(2,1)}, u32[]{:S(2)}) copy-start(bf16[2048,768]{1,0:T(8,128)(2,1)} %param.5) | copy-start | bytes 9437188
  8.1 0.6 copy-start.7
  8.7 0.8 copy-start.5
  8.8 3.2 %copy-start.9 = (pred[160]{0:T(512)(128)(4,1)}, pred[160]{0:T(512)(128)(4,1)S(1)}, u32[]{:S(2)}) copy-start(pred[160]{0:T(512)(128)(4,1)S(1)} %reshape.434) | copy-start | bytes 484
  10.4 0.6 copy-start.2
  12.1 13.7 %all-to-all-start = ((s32[8,1,2]{2,1,0:T(1,128)}), s32[8,1,2]{2,1,0:T(1,128)S(1)}, u32[]{:S(2)}, u32[]{:S(2)}) async-start(s32[8,1,2]{2,1,0:T(1,128)} %copy.92), calls=%async_computation | async-start | bytes 8192 | tf_op jit(solution)/shard_map/all_to_all | solution.py:81
  41.1 4.5 %copy-start.6 = (pred[16,10]{1,0:T(8,128)(4,1)S(1)}, pred[16,10]{1,0:T(8,128)(4,1)}, u32[]{:S(2)}) copy-start(pred[16,10]{1,0:T(8,128)(4,1)} %copy-done.5) | copy-start | bytes 484
  41.1 4.7 %copy-start.3 = (s32[160]{0:T(256)S(1)}, s32[160]{0:T(256)}, u32[]{:S(2)}) copy-start(s32[160]{0:T(256)} %copy-done.2) | copy-start | bytes 1924
  41.1 4.7 %copy-start.10 = (pred[160]{0:T(512)(128)(4,1)S(1)}, pred[160]{0:T(512)(128)(4,1)}, u32[]{:S(2)}) copy-start(pred[160]{0:T(512)(128)(4,1)} %copy-done.9) | copy-start | bytes 484
  41.2 6.7 %copy-start.4 = (s32[16,9]{1,0:T(8,128)S(1)}, s32[16,9]{1,0:T(8,128)}, u32[]{:S(2)}) copy-start(s32[16,9]{1,0:T(8,128)} %param.8) | copy-start | bytes 1732
  41.2 6.7 %copy-start.8 = (pred[16,9]{1,0:T(8,128)(4,1)S(1)}, pred[16,9]{1,0:T(8,128)(4,1)}, u32[]{:S(2)}) copy-start(pred[16,9]{1,0:T(8,128)(4,1)} %copy-done.7) | copy-start | bytes 436
  41.2 74.0 %all-to-all-start.1 = ((bf16[8,2,128,768]{3,2,1,0:T(8,128)(2,1)}), bf16[8,2,128,768]{3,2,1,0:T(8,128)(2,1)}, u32[]{:S(2)}, u32[]{:S(2)}) async-start(bf16[8,2,128,768]{3,2,1,0:T(8,128)(2,1)} %select_select_fusion), calls=%async_computation.1 | async-start | bytes 6291456 | tf_op jit(solution)/shard_map/all_to_all | solution.py:89
  116.4 14.0 %slice-start = ((s8[16777216]{0:T(1024)(128)(4,1)}), s8[4194304]{0:T(1024)(128)(4,1)S(1)}, s32[]{:S(2)}) async-start(s8[16777216]{0:T(1024)(128)(4,1)} %bitcast.58), calls=%async_computation.4 | async-start | bytes 8388608
  116.4 14.0 %slice-start.1 = ((s8[16777216]{0:T(1024)(128)(4,1)}), s8[4194304]{0:T(1024)(128)(4,1)S(1)}, s32[]{:S(2)}) async-start(s8[16777216]{0:T(1024)(128)(4,1)} %bitcast.58), calls=%async_computation.5 | async-start | bytes 8388608
  116.4 14.0 %slice-start.2 = ((s8[16777216]{0:T(1024)(128)(4,1)}), s8[4194304]{0:T(1024)(128)(4,1)S(1)}, s32[]{:S(2)}) async-start(s8[16777216]{0:T(1024)(128)(4,1)} %bitcast.58), calls=%async_computation.6 | async-start | bytes 8388608
  116.4 14.0 %slice-start.3 = ((s8[16777216]{0:T(1024)(128)(4,1)}), s8[4194304]{0:T(1024)(128)(4,1)S(1)}, s32[]{:S(2)}) async-start(s8[16777216]{0:T(1024)(128)(4,1)} %bitcast.58), calls=%async_computation.7 | async-start | bytes 8388608
  169.6 76.7 %all-to-all-start.2 = ((bf16[32,2,32,768]{3,2,1,0:T(8,128)(2,1)}), bf16[32,2,32,768]{3,2,1,0:T(8,128)(2,1)S(1)}, u32[]{:S(2)}, u32[]{:S(2)}) async-start(bf16[32,2,32,768]{3,2,1,0:T(8,128)(2,1)} %bitcast.63), calls=%async_computation.2 | async-start | bytes 6291456 | tf_op jit(solution)/shard_map/all_to_all | solution.py:97
  173.2 93.8 %all-gather.3.cloned.1.call-start = ((), (), s32[]{:S(2)}) async-start(), calls=%async_computation.3 | async-start | bytes 1966080 | tf_op jit(solution)/shard_map/all_gather | solution.py:112
  249.5 21.0 %copy-start.1 = (bf16[2048,768]{1,0:T(8,128)(2,1)S(1)}, bf16[2048,768]{1,0:T(8,128)(2,1)}, u32[]{:S(2)}) copy-start(bf16[2048,768]{1,0:T(8,128)(2,1)} %param.5) | copy-start | bytes 9437188
Sparse Core Ops, SparseCore 0:
  249.6 17.3 all-gather.2

commit v4 on v3

--- a/solution.py
+++ b/solution.py
@@ -1,8 +1,11 @@
+import functools
 import math
 
 import jax
 import jax.numpy as jnp
 from jax import lax
+from jax.experimental import pallas as pl
+from jax.experimental.pallas import tpu as pltpu
 from jax.sharding import PartitionSpec as P
 
 QROWS = 128
@@ -46,28 +49,116 @@
     return (slot_index, request)
 
 
+def pick_kernel(wanted, block_ref, out_ref):
+    out_ref[...] = block_ref[...]
+
+
+def pick_blocks(blocks, wanted):
+    _, rows, width = blocks.shape
+    return pl.pallas_call(
+        pick_kernel,
+        grid_spec=pltpu.PrefetchScalarGridSpec(
+            num_scalar_prefetch=1,
+            grid=(wanted.shape[0],),
+            in_specs=[pl.BlockSpec((1, rows, width), lambda i, wanted: (wanted[i], 0, 0))],
+            out_specs=pl.BlockSpec((1, rows, width), lambda i, wanted: (i, 0, 0)),
+        ),
+        out_shape=jax.ShapeDtypeStruct((wanted.shape[0], rows, width), blocks.dtype),
+        name="pick",
+    )(wanted, blocks)
+
+
+def sum_kernel(places, piece_ref, out_ref, total):
+    total[...] = jnp.zeros_like(total)
+
+    def add(i, carry):
+        total[places[i]] += piece_ref[i].astype(jnp.float32)
+        return carry
+
+    lax.fori_loop(0, piece_ref.shape[0], add, 0)
+    out_ref[...] = total[...].astype(out_ref.dtype)
+
+
+def sum_pieces(pieces, places, shard_blocks):
+    count, part, width = pieces.shape
+    return pl.pallas_call(
+        sum_kernel,
+        grid_spec=pltpu.PrefetchScalarGridSpec(
+            num_scalar_prefetch=1,
+            grid=(1,),
+            in_specs=[pl.BlockSpec((count, part, width), lambda i, places: (0, 0, 0))],
+            out_specs=pl.BlockSpec((shard_blocks, part, width), lambda i, places: (0, 0, 0)),
+            scratch_shapes=[pltpu.VMEM((shard_blocks, part, width), jnp.float32)],
+        ),
+        out_shape=jax.ShapeDtypeStruct((shard_blocks, part, width), jnp.bfloat16),
+        compiler_params=pltpu.CompilerParams(vmem_limit_bytes=32 * 1024 * 1024),
+        name="sum_pieces",
+    )(places, pieces)
+
+
+def weight_kernel(per_tile, factor, positive_slot, query_ref, flat_ref, bias_ref, weight_ref, loss_ref, score_ref):
+    tile = pl.program_id(0)
+    score_ref[...] = lax.dot_general(
+        query_ref[...], flat_ref[...], (((1,), (1,)), ((), ())), preferred_element_type=jnp.float32
+    )
+    eye = lax.broadcasted_iota(jnp.int32, (QROWS, PROWS), 0) == lax.broadcasted_iota(
+        jnp.int32, (QROWS, PROWS), 1
+    )
+    for block in range(per_tile):
+        rows = slice(block * QROWS, (block + 1) * QROWS)
+        scores = score_ref[rows, :] * factor + bias_ref[block]
+        largest = jnp.max(scores, axis=1, keepdims=True)
+        powers = jnp.exp(scores - largest)
+        total = jnp.sum(powers, axis=1, keepdims=True)
+        inverse = 1.0 / total
+        log_total = largest + jnp.log(total)
+        weight_ref[rows, :] = (powers * inverse).astype(jnp.bfloat16)
+        start = pl.multiple_of(positive_slot[tile * per_tile + block] * PROWS, PROWS)
+        own = score_ref[rows, pl.ds(start, PROWS)] * factor
+        own_weight = jnp.exp(own - largest) * inverse - eye.astype(jnp.float32)
+        weight_ref[rows, pl.ds(start, PROWS)] = own_weight.astype(jnp.bfloat16)
+        loss_ref[block] = jnp.sum(jnp.where(eye, log_total - own, 0.0), axis=0, keepdims=True)
+
+
 def dense_pass(queries, fetched, slot_index, is_live, factor):
     block_total = slot_index.shape[0]
     slots = fetched.shape[0]
     width = queries.shape[1]
-    flat = fetched.reshape(slots * PROWS, width)
+    columns = slots * PROWS
+    flat = fetched.reshape(columns, width)
     slot_range = jnp.arange(slots, dtype=jnp.int32)
     used = jnp.any((slot_index[:, :, None] == slot_range) & is_live[:, :, None], axis=1)
-    positive = (slot_index[:, 0, None] == slot_range).astype(jnp.float32)
-    scores = jnp.einsum("qd,pd->qp", queries, flat, preferred_element_type=jnp.float32) * factor
-    scores = scores.reshape(block_total, QROWS, slots, PROWS)
-    scores = jnp.where(used[:, None, :, None], scores, -jnp.inf)
-    diagonal = jnp.eye(QROWS, PROWS, dtype=jnp.float32)
-    target = positive[:, None, :, None] * diagonal[None, :, None, :]
-    largest = jnp.max(scores, axis=(2, 3), keepdims=True)
-    log_total = largest + jnp.log(jnp.sum(jnp.exp(scores - largest), axis=(2, 3), keepdims=True))
-    hit = jnp.sum(jnp.where(target > 0, scores, 0.0), axis=(2, 3))
-    losses = log_total[:, :, 0, 0] - hit
-    weights = (jnp.exp(scores - log_total) - target).astype(jnp.bfloat16)
-    weights = weights.reshape(block_total * QROWS, slots * PROWS)
+    bias = jnp.where(used, 0.0, -jnp.inf).astype(jnp.float32)
+    bias = jnp.broadcast_to(bias[:, None, :, None], (block_total, 1, slots, PROWS))
+    bias = bias.reshape(block_total, 1, columns)
+    per_tile = math.gcd(block_total, 4)
+    weights, losses = pl.pallas_call(
+        functools.partial(weight_kernel, per_tile, factor),
+        grid_spec=pltpu.PrefetchScalarGridSpec(
+            num_scalar_prefetch=1,
+            grid=(block_total // per_tile,),
+            in_specs=[
+                pl.BlockSpec((per_tile * QROWS, width), lambda i, slot: (i, 0)),
+                pl.BlockSpec((columns, width), lambda i, slot: (0, 0)),
+                pl.BlockSpec((per_tile, 1, columns), lambda i, slot: (i, 0, 0)),
+            ],
+            out_specs=[
+                pl.BlockSpec((per_tile * QROWS, columns), lambda i, slot: (i, 0)),
+                pl.BlockSpec((per_tile, 1, QROWS), lambda i, slot: (i, 0, 0)),
+            ],
+            scratch_shapes=[pltpu.VMEM((per_tile * QROWS, columns), jnp.float32)],
+        ),
+        out_shape=[
+            jax.ShapeDtypeStruct((block_total * QROWS, columns), jnp.bfloat16),
+            jax.ShapeDtypeStruct((block_total, 1, QROWS), jnp.float32),
+        ],
+        compiler_params=pltpu.CompilerParams(vmem_limit_bytes=52 * 1024 * 1024),
+        name="weights",
+    )(slot_index[:, 0], queries, flat, bias)
+    slot_grads = jnp.einsum("qp,qd->pd", weights, queries, preferred_element_type=jnp.float32)
+    slot_grads, weights = lax.optimization_barrier((slot_grads.astype(jnp.bfloat16), weights))
     query_grad = jnp.einsum("qp,pd->qd", weights, flat, preferred_element_type=jnp.float32)
-    slot_grads = jnp.einsum("qp,qd->pd", weights, queries, preferred_element_type=jnp.float32)
-    return slot_grads.astype(jnp.bfloat16), (losses, query_grad.astype(jnp.bfloat16))
+    return slot_grads, (losses.reshape(block_total, QROWS), query_grad.astype(jnp.bfloat16))
 
 
 def body(queries, passages, positives, mined_blocks, counts):
@@ -81,10 +172,7 @@
     wanted = lax.all_to_all(request, "dev", split_axis=0, concat_axis=0, tiled=True)
     asked = lax.all_gather(wanted, "grp", axis=0, tiled=False)
     blocks = passages.reshape(shard_blocks, PROWS, width)
-    picks = wanted.reshape(-1)[:, None, None]
-    outgoing = jnp.broadcast_to(blocks[0][None], (owners * CAP, PROWS, width))
-    for local in range(1, shard_blocks):
-        outgoing = jnp.where(picks == local, blocks[local][None], outgoing)
+    outgoing = pick_blocks(blocks, wanted.reshape(-1))
     outgoing = outgoing.reshape(owners, CAP, PROWS, width)
     fetched = lax.all_to_all(outgoing, "dev", split_axis=0, concat_axis=0, tiled=True).reshape(
         owners * CAP, PROWS, width
@@ -101,14 +189,8 @@
         concat_axis=0,
         tiled=True,
     )
-    place = (jnp.arange(shard_blocks, dtype=jnp.int32)[:, None] == asked.reshape(-1)).astype(jnp.bfloat16)
-    share = jnp.einsum(
-        "bs,sd->bd",
-        place,
-        returned.reshape(groups * owners * CAP, part * width),
-        preferred_element_type=jnp.float32,
-    )
-    share = share.astype(jnp.bfloat16).reshape(shard_blocks, part, width)
+    pieces = returned.reshape(groups * owners * CAP, part, width)
+    share = sum_pieces(pieces, asked.reshape(-1), shard_blocks)
     gathered = lax.all_gather(share, "grp", axis=0, tiled=False)
     passage_grad = gathered.transpose(1, 0, 2, 3).reshape(shard_blocks * PROWS, width)
     passage_grad = passage_grad.astype(jnp.float32)

time: 278 us -> 247 us (0.89)
  other arithmetic: 48 us -> 5.49 us
  Pallas kernels: 0 us -> 29.2 us
  matrix products: 35.2 us -> 20.4 us
  blocking collectives: 19.6 us -> 33.1 us
  local copies, waits for them, and re-layouts: 23.4 us -> 9.97 us
  starting transfers between devices: 15.4 us -> 7.39 us
  waiting for transfers between devices: 121 us -> 126 us
    pallas_call x0 -> x3, Pallas kernels: none -> 29.2 us  [the longest x1 16.5 us: dense_pass(): pl.pallas_call(functools.partial(weight_kernel, per_tile, factor), grid_s...]
    convert_element_type x3 -> x0, other arithmetic: 14.8 us -> none  [the longest x1 14.8 us: dense_pass(): weights = (jnp.exp(scores - log_total) - target).astype(jnp.bfloat16)]
    dot_general x2 -> x0, matrix products: 14.5 us -> none  [the longest x1 14 us: dense_pass(): jnp.einsum('qd,pd->qp', queries, flat, preferred_element_type=jnp.float32)]
    all_to_all x0 -> x1, blocking collectives: none -> 13.5 us  [body(): lax.all_to_all(request, 'dev', split_axis=0, concat_axis=0, tiled=True)]
    reduce_sum x1 -> x0, other arithmetic: 12.8 us -> none  [dense_pass(): hit = jnp.sum(jnp.where(target > 0, scores, 0.0), axis=(2, 3))]
    eq x8 -> x0, local copies, waits for them, and re-layouts: 9.18 us -> none  [the longest x7 9.08 us: body(): outgoing = jnp.where(picks == local, blocks[local][None], outgoing)]
    all_to_all x1, waiting for transfers between devices: 59.5 us -> 67 us  [body(): lax.all_to_all(outgoing, 'dev', split_axis=0, concat_axis=0, tiled=True)]
    mul x1 -> x0, other arithmetic: 7.38 us -> none  [dense_pass(): target = positive[:, None, :, None] * diagonal[None, :, None, :]]
  transfers between devices with their start and end apart: 4 -> 3, of which waited for: 4 -> 3; matrix products, arithmetic and copies ran while one was open for 9% -> 6% of each run, Pallas kernels for 0% -> 0%
where the time goes in v4:
time: 247 us; the launch traced here: 246 us
  waiting for transfers between devices  126 us (51%)
  blocking collectives  33.1 us (13%)
  Pallas kernels  29.2 us (12%)
  matrix products  20.4 us (8%)
  between operations  14.2 us (6%)
  local copies, waits for them, and re-layouts  9.97 us (4%)
  starting transfers between devices  7.39 us (3%)
  other arithmetic  5.49 us (2%)
    all_to_all x1, waiting for transfers between devices, body(): lax.all_to_all(outgoing, 'dev', split_axis=0, concat_axis=0, tiled=True)  67 us
    all_to_all x1, waiting for transfers between devices, body(): lax.all_to_all(sending.reshape(groups * owners, CAP, part, width), ('grp'...  52.7 us
    all_gather x1, blocking collectives, body(): asked = lax.all_gather(wanted, 'grp', axis=0, tiled=False)  19.6 us
    pallas_call x1, Pallas kernels, dense_pass(): pl.pallas_call(functools.partial(weight_kernel, per_tile, factor), grid_s...  16.5 us
    all_to_all x1, blocking collectives, body(): lax.all_to_all(request, 'dev', split_axis=0, concat_axis=0, tiled=True)  13.5 us
    dot_general x1, matrix products, dense_pass(): jnp.einsum('qp,pd->qd', weights, flat, preferred_element_type=jnp.float32)  11.2 us
    pallas_call x1, Pallas kernels, pick_blocks(): pl.pallas_call(pick_kernel, grid_spec=pltpu.PrefetchScalarGridSpec(num_sc...  10.5 us
    dot_general x1, matrix products, dense_pass(): jnp.einsum('qp,qd->pd', weights, queries, preferred_element_type=jnp.floa...  9.27 us
  transfers between devices with their start and end apart: 3, of which 3 were waited for; matrix products, arithmetic and copies ran while one was open for 6% of the time, Pallas kernels for 0%

profile of v4, /device:TPU:0, one launch (start us, length us, event | category | flops | bytes accessed | tf_op | source)
XLA Modules:
  0.0 245.9 jit_solution(13305112205515186779)
XLA Ops:
  7.2 0.7 iota_compare_fusion.3
  8.0 0.1 reshape.290
  8.1 0.7 copy.22
  8.8 0.8 pad_add_fusion
  9.7 0.2 fusion.2
  9.9 0.2 convert_reduce_fusion
  10.1 0.1 select_reduce_fusion.1
  10.4 13.5 %all_to_all.19 = s32[8,1,2]{2,1,0:T(1,128)S(1)} all-to-all(s32[8,1,2]{2,1,0:T(1,128)S(1)} %copy.23), channel_id=1, replica_groups=mesh['grp'=4,'dev'=8] {'dev'}, dimensions={0} | all-to-all | bytes 128 | tf_op jit(solution)/shard_map/all_to_all | solution.py:172
  23.9 0.5 broadcast.258
  24.4 0.6 reduce.8
  25.0 0.6 reshape.292.wanted
  25.6 10.5 %pick.1 = bf16[16,128,768]{2,1,0:T(8,128)(2,1)} custom-call(s32[16]{0:T(128)} %reshape.292.wanted, bf16[8,128,768]{2,1,0:T(8,128)(2,1)} %bitcast.31), custom_call_target="tpu_custom_call" | custom-call | tf_op jit(solution)/shard_map/pick/pallas_call | solution.py:58
  36.1 3.8 %all-to-all-start.1 = ((bf16[8,2,128,768]{3,2,1,0:T(8,128)(2,1)}), bf16[8,2,128,768]{3,2,1,0:T(8,128)(2,1)S(1)}, u32[]{:S(2)}, u32[]{:S(2)}) async-start(bf16[8,2,128,768]{3,2,1,0:T(8,128)(2,1)} %bitcast.27), calls=%async_computation.1 | async-start | bytes 6291456 | tf_op jit(solution)/shard_map/all_to_all | solution.py:177
  40.0 0.2 select_reduce_fusion
  40.3 1.6 gather_fusion
  42.1 0.1 slice_reduce_fusion.positive_slot
  42.3 0.1 fusion.4
  42.4 67.0 %all-to-all-done.1 = bf16[8,2,128,768]{3,2,1,0:T(8,128)(2,1)S(1)} async-done(((bf16[8,2,128,768]{3,2,1,0:T(8,128)(2,1)}), bf16[8,2,128,768]{3,2,1,0:T(8,128)(2,1)S(1)}, u32[]{:S(2)}, u32[]{:S(2)}) %all-to-all-start.1) | async-done | bytes 3145760 | tf_op jit(solution)/shard_map/all_to_all | solution.py:177
  109.5 1.6 copy-done
  111.1 16.5 %weights.1 = (bf16[2048,2048]{1,0:T(8,128)(2,1)}, f32[16,1,128]{2,1,0:T(1,128)}) custom-call(s32[16]{0:T(128)S(1)} %slice_reduce_fusion.positive_slot, bf16[2048,768]{1,0:T(8,128)(2,1)} %query_ref.1, bf16[2048,768]{1,0:T(8,128)(2,1)} %bitcast.25, f32[16,1,2048]{2,1,0:T(1,128)S(1)} %bitcast.24), custom_call_target="tpu_custom_call" | custom-call | tf_op jit(solution)/shard_map/weights/pallas_call | solution.py:135
  127.6 9.3 %convolution_convert_fusion.1 = bf16[2048,768]{1,0:T(8,128)(2,1)S(1)} fusion(bf16[2048,2048]{1,0:T(8,128)(2,1)} %get-tuple-element.9, bf16[2048,768]{1,0:T(8,128)(2,1)S(1)} %copy-done.1), kind=kOutput, calls=%fused_computation.2 | convolution fusion | flops 6444023808 | bytes 14680064 | tf_op jit(solution)/shard_map/qp,qd->pd/dot_general | solution.py:158
  136.8 2.0 copy.26
  138.8 3.6 %all-to-all-start.2 = ((bf16[32,2,32,768]{3,2,1,0:T(8,128)(2,1)}), bf16[32,2,32,768]{3,2,1,0:T(8,128)(2,1)S(1)}, u32[]{:S(2)}, u32[]{:S(2)}) async-start(bf16[32,2,32,768]{3,2,1,0:T(8,128)(2,1)} %bitcast.28), calls=%async_computation.2 | async-start | bytes 6291456 | tf_op jit(solution)/shard_map/all_to_all | solution.py:185
  142.4 19.6 %all-gather = s32[32,1,2]{2,1,0:T(1,128)S(1)} all-gather(s32[8,1,2]{2,1,0:T(1,128)S(1)} %all_to_all.19), channel_id=2, replica_groups=mesh['grp'=4,'dev'=8] {'grp'}, dimensions={0}, use_global_device_ids=true | all-gather | bytes 320 | tf_op jit(solution)/shard_map/all_gather | solution.py:173
  162.0 0.6 reduce.9
  162.6 0.1 reshape.296.places
  162.7 52.7 %all-to-all-done.2 = bf16[32,2,32,768]{3,2,1,0:T(8,128)(2,1)S(1)} async-done(((bf16[32,2,32,768]{3,2,1,0:T(8,128)(2,1)}), bf16[32,2,32,768]{3,2,1,0:T(8,128)(2,1)S(1)}, u32[]{:S(2)}, u32[]{:S(2)}) %all-to-all-start.2) | async-done | bytes 3145760 | tf_op jit(solution)/shard_map/all_to_all | solution.py:185
  215.4 2.2 sum_pieces.1
  217.7 11.2 %convolution_convert_fusion = bf16[2048,768]{1,0:T(8,128)(2,1)} fusion(bf16[2048,2048]{1,0:T(8,128)(2,1)} %get-tuple-element.9, bf16[2048,768]{1,0:T(8,128)(2,1)} %bitcast.26), kind=kOutput, calls=%fused_computation.1 | convolution fusion | flops 6444023808 | bytes 14680064 | tf_op jit(solution)/shard_map/qp,pd->qd/dot_general | solution.py:160
  228.9 6.4 %all-gather.4.cloned.1.call-done = bf16[32,32,768]{2,1,0:T(8,128)(2,1)} async-done(((bf16[8,32,768]{2,1,0:T(8,128)(2,1)}), bf16[32,32,768]{2,1,0:T(8,128)(2,1)}) %all-gather.4.cloned.1.call-update) | async-done | bytes 1572880 | tf_op jit(solution)/shard_map/all_gather | solution.py:194
  235.2 1.8 convert_bitcast_fusion
  237.0 2.0 copy.27
  (23 shorter events, 0.9 us)
Async XLA Ops:
  36.1 5.9 %copy-start.2 = (s32[16,9]{1,0:T(8,128)S(1)}, s32[16,9]{1,0:T(8,128)}, u32[]{:S(2)}) copy-start(s32[16,9]{1,0:T(8,128)} %param.8) | copy-start | bytes 1732
  36.1 73.4 %all-to-all-start.1 = ((bf16[8,2,128,768]{3,2,1,0:T(8,128)(2,1)}), bf16[8,2,128,768]{3,2,1,0:T(8,128)(2,1)S(1)}, u32[]{:S(2)}, u32[]{:S(2)}) async-start(bf16[8,2,128,768]{3,2,1,0:T(8,128)(2,1)} %bitcast.27), calls=%async_computation.1 | async-start | bytes 6291456 | tf_op jit(solution)/shard_map/all_to_all | solution.py:177
  109.4 1.7 copy-start
  111.1 16.5 %copy-start.1 = (bf16[2048,768]{1,0:T(8,128)(2,1)S(1)}, bf16[2048,768]{1,0:T(8,128)(2,1)}, u32[]{:S(2)}) copy-start(bf16[2048,768]{1,0:T(8,128)(2,1)} %query_ref.1) | copy-start | bytes 9437188
  138.8 76.7 %all-to-all-start.2 = ((bf16[32,2,32,768]{3,2,1,0:T(8,128)(2,1)}), bf16[32,2,32,768]{3,2,1,0:T(8,128)(2,1)S(1)}, u32[]{:S(2)}, u32[]{:S(2)}) async-start(bf16[32,2,32,768]{3,2,1,0:T(8,128)(2,1)} %bitcast.28), calls=%async_computation.2 | async-start | bytes 6291456 | tf_op jit(solution)/shard_map/all_to_all | solution.py:185
  142.4 92.9 %all-gather.4.cloned.1.call-start = ((), (), s32[]{:S(2)}) async-start(), calls=%async_computation.3 | async-start | bytes 1966080 | tf_op jit(solution)/shard_map/all_gather | solution.py:194
Sparse Core Ops, SparseCore 0:
  217.8 17.3 all-gather.3

commit v5 on v4

--- a/solution.py
+++ b/solution.py
@@ -49,21 +49,26 @@
     return (slot_index, request)
 
 
-def pick_kernel(wanted, block_ref, out_ref):
-    out_ref[...] = block_ref[...]
+def pick_kernel(per_step, wanted, block_ref, out_ref):
+    step = pl.program_id(0)
+    for place in range(per_step):
+        out_ref[place] = block_ref[wanted[step * per_step + place]]
 
 
 def pick_blocks(blocks, wanted):
-    _, rows, width = blocks.shape
+    held, rows, width = blocks.shape
+    count = wanted.shape[0]
+    per_step = math.gcd(count, 4)
     return pl.pallas_call(
-        pick_kernel,
+        functools.partial(pick_kernel, per_step),
         grid_spec=pltpu.PrefetchScalarGridSpec(
             num_scalar_prefetch=1,
-            grid=(wanted.shape[0],),
-            in_specs=[pl.BlockSpec((1, rows, width), lambda i, wanted: (wanted[i], 0, 0))],
-            out_specs=pl.BlockSpec((1, rows, width), lambda i, wanted: (i, 0, 0)),
-        ),
-        out_shape=jax.ShapeDtypeStruct((wanted.shape[0], rows, width), blocks.dtype),
+            grid=(count // per_step,),
+            in_specs=[pl.BlockSpec((held, rows, width), lambda i, wanted: (0, 0, 0))],
+            out_specs=pl.BlockSpec((per_step, rows, width), lambda i, wanted: (i, 0, 0)),
+        ),
+        out_shape=jax.ShapeDtypeStruct((count, rows, width), blocks.dtype),
+        compiler_params=pltpu.CompilerParams(vmem_limit_bytes=16 * 1024 * 1024),
         name="pick",
     )(wanted, blocks)
 

time: 247 us -> 239 us (0.968)
  Pallas kernels: 29.2 us -> 21.4 us
    pallas_call x1, Pallas kernels: 10.5 us -> 2.68 us  [pick_blocks(): pl.pallas_call(functools.partial(pick_kernel, per_step), grid_spec=pltpu....]
where the time goes in v5:
time: 239 us
  waiting for transfers between devices  126 us (53%)
  blocking collectives  33.1 us (14%)
  Pallas kernels  21.4 us (9%)
  matrix products  20.4 us (9%)
  between operations  14.2 us (6%)
  local copies, waits for them, and re-layouts  10.9 us (5%)
  starting transfers between devices  7.46 us (3%)
  other arithmetic  5.49 us (2%)
    all_to_all x1, waiting for transfers between devices, body(): lax.all_to_all(outgoing, 'dev', split_axis=0, concat_axis=0, tiled=True)  66.9 us
    all_to_all x1, waiting for transfers between devices, body(): lax.all_to_all(sending.reshape(groups * owners, CAP, part, width), ('grp'...  52.7 us
    all_gather x1, blocking collectives, body(): asked = lax.all_gather(wanted, 'grp', axis=0, tiled=False)  19.6 us
    pallas_call x1, Pallas kernels, dense_pass(): pl.pallas_call(functools.partial(weight_kernel, per_tile, factor), grid_s...  16.5 us
    all_to_all x1, blocking collectives, body(): lax.all_to_all(request, 'dev', split_axis=0, concat_axis=0, tiled=True)  13.5 us
    dot_general x1, matrix products, dense_pass(): jnp.einsum('qp,pd->qd', weights, flat, preferred_element_type=jnp.float32)  11.2 us
    dot_general x1, matrix products, dense_pass(): jnp.einsum('qp,qd->pd', weights, queries, preferred_element_type=jnp.floa...  9.25 us
    all_gather x1, waiting for transfers between devices, body(): gathered = lax.all_gather(share, 'grp', axis=0, tiled=False)  6.39 us
  transfers between devices with their start and end apart: 3, of which 3 were waited for; matrix products, arithmetic and copies ran while one was open for 6% of the time, Pallas kernels for 0%

profile of v5, /device:TPU:0, one launch (start us, length us, event | category | flops | bytes accessed | tf_op | source)
XLA Modules:
  0.0 238.9 jit_solution(16582065605714755721)
XLA Ops:
  7.2 0.7 iota_compare_fusion.3
  8.0 0.1 reshape.290
  8.1 0.7 copy.22
  8.8 0.8 pad_add_fusion
  9.7 0.2 fusion.2
  9.9 0.2 convert_reduce_fusion
  10.1 0.1 select_reduce_fusion.1
  10.4 13.5 %all_to_all.19 = s32[8,1,2]{2,1,0:T(1,128)S(1)} all-to-all(s32[8,1,2]{2,1,0:T(1,128)S(1)} %copy.23), channel_id=1, replica_groups=mesh['grp'=4,'dev'=8] {'dev'}, dimensions={0} | all-to-all | bytes 128 | tf_op jit(solution)/shard_map/all_to_all | solution.py:177
  23.9 0.5 broadcast.258
  24.4 0.6 reduce.8
  25.1 1.4 copy-done
  26.5 2.7 %pick.1 = bf16[16,128,768]{2,1,0:T(8,128)(2,1)} custom-call(s32[16]{0:T(128)S(1)} %reshape.292.wanted, bf16[8,128,768]{2,1,0:T(8,128)(2,1)S(1)} %bitcast.24), custom_call_target="tpu_custom_call" | custom-call | tf_op jit(solution)/shard_map/pick/pallas_call | solution.py:62
  29.2 3.8 %all-to-all-start.1 = ((bf16[8,2,128,768]{3,2,1,0:T(8,128)(2,1)}), bf16[8,2,128,768]{3,2,1,0:T(8,128)(2,1)S(1)}, u32[]{:S(2)}, u32[]{:S(2)}) async-start(bf16[8,2,128,768]{3,2,1,0:T(8,128)(2,1)} %bitcast.5), calls=%async_computation.1 | async-start | bytes 6291456 | tf_op jit(solution)/shard_map/all_to_all | solution.py:182
  33.1 0.2 select_reduce_fusion
  33.4 1.6 gather_fusion
  35.3 0.1 slice_reduce_fusion.positive_slot
  35.4 0.1 fusion.4
  35.5 66.9 %all-to-all-done.1 = bf16[8,2,128,768]{3,2,1,0:T(8,128)(2,1)S(1)} async-done(((bf16[8,2,128,768]{3,2,1,0:T(8,128)(2,1)}), bf16[8,2,128,768]{3,2,1,0:T(8,128)(2,1)S(1)}, u32[]{:S(2)}, u32[]{:S(2)}) %all-to-all-start.1) | async-done | bytes 3145760 | tf_op jit(solution)/shard_map/all_to_all | solution.py:182
  102.5 1.6 copy-done.1
  104.1 16.5 %weights.1 = (bf16[2048,2048]{1,0:T(8,128)(2,1)}, f32[16,1,128]{2,1,0:T(1,128)}) custom-call(s32[16]{0:T(128)S(1)} %slice_reduce_fusion.positive_slot, bf16[2048,768]{1,0:T(8,128)(2,1)} %query_ref.1, bf16[2048,768]{1,0:T(8,128)(2,1)} %bitcast.26, f32[16,1,2048]{2,1,0:T(1,128)S(1)} %bitcast.25), custom_call_target="tpu_custom_call" | custom-call | tf_op jit(solution)/shard_map/weights/pallas_call | solution.py:140
  120.6 9.3 %convolution_convert_fusion.1 = bf16[2048,768]{1,0:T(8,128)(2,1)S(1)} fusion(bf16[2048,2048]{1,0:T(8,128)(2,1)} %get-tuple-element.9, bf16[2048,768]{1,0:T(8,128)(2,1)S(1)} %copy-done.2), kind=kOutput, calls=%fused_computation.2 | convolution fusion | flops 6444023808 | bytes 14680064 | tf_op jit(solution)/shard_map/qp,qd->pd/dot_general | solution.py:163
  129.8 2.0 copy.26
  131.8 3.6 %all-to-all-start.2 = ((bf16[32,2,32,768]{3,2,1,0:T(8,128)(2,1)}), bf16[32,2,32,768]{3,2,1,0:T(8,128)(2,1)S(1)}, u32[]{:S(2)}, u32[]{:S(2)}) async-start(bf16[32,2,32,768]{3,2,1,0:T(8,128)(2,1)} %bitcast.28), calls=%async_computation.2 | async-start | bytes 6291456 | tf_op jit(solution)/shard_map/all_to_all | solution.py:190
  135.5 19.6 %all-gather = s32[32,1,2]{2,1,0:T(1,128)S(1)} all-gather(s32[8,1,2]{2,1,0:T(1,128)S(1)} %all_to_all.19), channel_id=2, replica_groups=mesh['grp'=4,'dev'=8] {'grp'}, dimensions={0}, use_global_device_ids=true | all-gather | bytes 320 | tf_op jit(solution)/shard_map/all_gather | solution.py:178
  155.1 0.6 reduce.9
  155.7 0.1 reshape.296.places
  155.8 52.7 %all-to-all-done.2 = bf16[32,2,32,768]{3,2,1,0:T(8,128)(2,1)S(1)} async-done(((bf16[32,2,32,768]{3,2,1,0:T(8,128)(2,1)}), bf16[32,2,32,768]{3,2,1,0:T(8,128)(2,1)S(1)}, u32[]{:S(2)}, u32[]{:S(2)}) %all-to-all-start.2) | async-done | bytes 3145760 | tf_op jit(solution)/shard_map/all_to_all | solution.py:190
  208.5 2.2 sum_pieces.1
  210.7 11.2 %convolution_convert_fusion = bf16[2048,768]{1,0:T(8,128)(2,1)} fusion(bf16[2048,2048]{1,0:T(8,128)(2,1)} %get-tuple-element.9, bf16[2048,768]{1,0:T(8,128)(2,1)} %bitcast.27), kind=kOutput, calls=%fused_computation.1 | convolution fusion | flops 6444023808 | bytes 14680064 | tf_op jit(solution)/shard_map/qp,pd->qd/dot_general | solution.py:165
  221.9 6.4 %all-gather.4.cloned.1.call-done = bf16[32,32,768]{2,1,0:T(8,128)(2,1)} async-done(((bf16[8,32,768]{2,1,0:T(8,128)(2,1)}), bf16[32,32,768]{2,1,0:T(8,128)(2,1)}) %all-gather.4.cloned.1.call-update) | async-done | bytes 1572880 | tf_op jit(solution)/shard_map/all_gather | solution.py:199
  228.3 1.8 convert_bitcast_fusion
  230.1 2.0 copy.27
  (25 shorter events, 1.0 us)
Async XLA Ops:
  25.1 1.4 copy-start
  29.2 5.9 %copy-start.3 = (s32[16,9]{1,0:T(8,128)S(1)}, s32[16,9]{1,0:T(8,128)}, u32[]{:S(2)}) copy-start(s32[16,9]{1,0:T(8,128)} %param.8) | copy-start | bytes 1732
  29.2 73.3 %all-to-all-start.1 = ((bf16[8,2,128,768]{3,2,1,0:T(8,128)(2,1)}), bf16[8,2,128,768]{3,2,1,0:T(8,128)(2,1)S(1)}, u32[]{:S(2)}, u32[]{:S(2)}) async-start(bf16[8,2,128,768]{3,2,1,0:T(8,128)(2,1)} %bitcast.5), calls=%async_computation.1 | async-start | bytes 6291456 | tf_op jit(solution)/shard_map/all_to_all | solution.py:182
  102.4 1.7 copy-start.1
  104.1 16.5 %copy-start.2 = (bf16[2048,768]{1,0:T(8,128)(2,1)S(1)}, bf16[2048,768]{1,0:T(8,128)(2,1)}, u32[]{:S(2)}) copy-start(bf16[2048,768]{1,0:T(8,128)(2,1)} %query_ref.1) | copy-start | bytes 9437188
  131.8 76.7 %all-to-all-start.2 = ((bf16[32,2,32,768]{3,2,1,0:T(8,128)(2,1)}), bf16[32,2,32,768]{3,2,1,0:T(8,128)(2,1)S(1)}, u32[]{:S(2)}, u32[]{:S(2)}) async-start(bf16[32,2,32,768]{3,2,1,0:T(8,128)(2,1)} %bitcast.28), calls=%async_computation.2 | async-start | bytes 6291456 | tf_op jit(solution)/shard_map/all_to_all | solution.py:190
  135.4 92.9 %all-gather.4.cloned.1.call-start = ((), (), s32[]{:S(2)}) async-start(), calls=%async_computation.3 | async-start | bytes 1966080 | tf_op jit(solution)/shard_map/all_gather | solution.py:199
Sparse Core Ops, SparseCore 0:
  210.9 17.3 all-gather.3

commit v6 on v5

--- a/solution.py
+++ b/solution.py
@@ -103,9 +103,11 @@
 
 def weight_kernel(per_tile, factor, positive_slot, query_ref, flat_ref, bias_ref, weight_ref, loss_ref, score_ref):
     tile = pl.program_id(0)
-    score_ref[...] = lax.dot_general(
-        query_ref[...], flat_ref[...], (((1,), (1,)), ((), ())), preferred_element_type=jnp.float32
-    )
+    for first in range(0, per_tile, 2):
+        pair = slice(first * QROWS, min(first + 2, per_tile) * QROWS)
+        score_ref[pair, :] = lax.dot_general(
+            query_ref[pair, :], flat_ref[...], (((1,), (1,)), ((), ())), preferred_element_type=jnp.float32
+        )
     eye = lax.broadcasted_iota(jnp.int32, (QROWS, PROWS), 0) == lax.broadcasted_iota(
         jnp.int32, (QROWS, PROWS), 1
     )

time: 239 us -> 239 us (level)
  no operation moved by 1% of the time
where the time goes in v6:
time: 239 us; the launch traced here: 238 us
  waiting for transfers between devices  126 us (53%)
  blocking collectives  33.1 us (14%)
  Pallas kernels  20.7 us (9%)
  matrix products  20.4 us (9%)
  between operations  14.2 us (6%)
  local copies, waits for them, and re-layouts  10.9 us (5%)
  starting transfers between devices  7.46 us (3%)
  other arithmetic  5.49 us (2%)
    all_to_all x1, waiting for transfers between devices, body(): lax.all_to_all(outgoing, 'dev', split_axis=0, concat_axis=0, tiled=True)  66.9 us
    all_to_all x1, waiting for transfers between devices, body(): lax.all_to_all(sending.reshape(groups * owners, CAP, part, width), ('grp'...  52.7 us
    all_gather x1, blocking collectives, body(): asked = lax.all_gather(wanted, 'grp', axis=0, tiled=False)  19.6 us
    pallas_call x1, Pallas kernels, dense_pass(): pl.pallas_call(functools.partial(weight_kernel, per_tile, factor), grid_s...  15.8 us
    all_to_all x1, blocking collectives, body(): lax.all_to_all(request, 'dev', split_axis=0, concat_axis=0, tiled=True)  13.5 us
    dot_general x1, matrix products, dense_pass(): jnp.einsum('qp,pd->qd', weights, flat, preferred_element_type=jnp.float32)  11.2 us
    dot_general x1, matrix products, dense_pass(): jnp.einsum('qp,qd->pd', weights, queries, preferred_element_type=jnp.floa...  9.25 us
    all_gather x1, waiting for transfers between devices, body(): gathered = lax.all_gather(share, 'grp', axis=0, tiled=False)  6.39 us
  transfers between devices with their start and end apart: 3, of which 3 were waited for; matrix products, arithmetic and copies ran while one was open for 6% of the time, Pallas kernels for 0%

profile of v6, /device:TPU:0, one launch (start us, length us, event | category | flops | bytes accessed | tf_op | source)
XLA Modules:
  0.0 238.3 jit_solution(4140473404403526966)
XLA Ops:
  7.2 0.7 iota_compare_fusion.3
  8.0 0.1 reshape.290
  8.1 0.7 copy.22
  8.8 0.8 pad_add_fusion
  9.7 0.2 fusion.2
  9.9 0.2 convert_reduce_fusion
  10.1 0.1 select_reduce_fusion.1
  10.4 13.5 %all_to_all.19 = s32[8,1,2]{2,1,0:T(1,128)S(1)} all-to-all(s32[8,1,2]{2,1,0:T(1,128)S(1)} %copy.23), channel_id=1, replica_groups=mesh['grp'=4,'dev'=8] {'dev'}, dimensions={0} | all-to-all | bytes 128 | tf_op jit(solution)/shard_map/all_to_all | solution.py:179
  23.9 0.5 broadcast.258
  24.4 0.6 reduce.8
  25.1 1.4 copy-done
  26.5 2.7 %pick.1 = bf16[16,128,768]{2,1,0:T(8,128)(2,1)} custom-call(s32[16]{0:T(128)S(1)} %reshape.292.wanted, bf16[8,128,768]{2,1,0:T(8,128)(2,1)S(1)} %bitcast.24), custom_call_target="tpu_custom_call" | custom-call | tf_op jit(solution)/shard_map/pick/pallas_call | solution.py:62
  29.2 3.8 %all-to-all-start.1 = ((bf16[8,2,128,768]{3,2,1,0:T(8,128)(2,1)}), bf16[8,2,128,768]{3,2,1,0:T(8,128)(2,1)S(1)}, u32[]{:S(2)}, u32[]{:S(2)}) async-start(bf16[8,2,128,768]{3,2,1,0:T(8,128)(2,1)} %bitcast.5), calls=%async_computation.1 | async-start | bytes 6291456 | tf_op jit(solution)/shard_map/all_to_all | solution.py:184
  33.1 0.2 select_reduce_fusion
  33.4 1.6 gather_fusion
  35.3 0.1 slice_reduce_fusion.positive_slot
  35.4 0.1 fusion.4
  35.5 66.9 %all-to-all-done.1 = bf16[8,2,128,768]{3,2,1,0:T(8,128)(2,1)S(1)} async-done(((bf16[8,2,128,768]{3,2,1,0:T(8,128)(2,1)}), bf16[8,2,128,768]{3,2,1,0:T(8,128)(2,1)S(1)}, u32[]{:S(2)}, u32[]{:S(2)}) %all-to-all-start.1) | async-done | bytes 3145760 | tf_op jit(solution)/shard_map/all_to_all | solution.py:184
  102.5 1.6 copy-done.1
  104.1 15.8 %weights.1 = (bf16[2048,2048]{1,0:T(8,128)(2,1)}, f32[16,1,128]{2,1,0:T(1,128)}) custom-call(s32[16]{0:T(128)S(1)} %slice_reduce_fusion.positive_slot, bf16[2048,768]{1,0:T(8,128)(2,1)} %query_ref.1, bf16[2048,768]{1,0:T(8,128)(2,1)} %bitcast.26, f32[16,1,2048]{2,1,0:T(1,128)S(1)} %bitcast.25), custom_call_target="tpu_custom_call" | custom-call | tf_op jit(solution)/shard_map/weights/pallas_call | solution.py:142
  119.9 9.3 %convolution_convert_fusion.1 = bf16[2048,768]{1,0:T(8,128)(2,1)S(1)} fusion(bf16[2048,2048]{1,0:T(8,128)(2,1)} %get-tuple-element.9, bf16[2048,768]{1,0:T(8,128)(2,1)S(1)} %copy-done.2), kind=kOutput, calls=%fused_computation.2 | convolution fusion | flops 6444023808 | bytes 14680064 | tf_op jit(solution)/shard_map/qp,qd->pd/dot_general | solution.py:165
  129.2 2.0 copy.26
  131.1 3.6 %all-to-all-start.2 = ((bf16[32,2,32,768]{3,2,1,0:T(8,128)(2,1)}), bf16[32,2,32,768]{3,2,1,0:T(8,128)(2,1)S(1)}, u32[]{:S(2)}, u32[]{:S(2)}) async-start(bf16[32,2,32,768]{3,2,1,0:T(8,128)(2,1)} %bitcast.28), calls=%async_computation.2 | async-start | bytes 6291456 | tf_op jit(solution)/shard_map/all_to_all | solution.py:192
  134.8 19.6 %all-gather = s32[32,1,2]{2,1,0:T(1,128)S(1)} all-gather(s32[8,1,2]{2,1,0:T(1,128)S(1)} %all_to_all.19), channel_id=2, replica_groups=mesh['grp'=4,'dev'=8] {'grp'}, dimensions={0}, use_global_device_ids=true | all-gather | bytes 320 | tf_op jit(solution)/shard_map/all_gather | solution.py:180
  154.4 0.6 reduce.9
  155.0 0.1 reshape.296.places
  155.1 52.7 %all-to-all-done.2 = bf16[32,2,32,768]{3,2,1,0:T(8,128)(2,1)S(1)} async-done(((bf16[32,2,32,768]{3,2,1,0:T(8,128)(2,1)}), bf16[32,2,32,768]{3,2,1,0:T(8,128)(2,1)S(1)}, u32[]{:S(2)}, u32[]{:S(2)}) %all-to-all-start.2) | async-done | bytes 3145760 | tf_op jit(solution)/shard_map/all_to_all | solution.py:192
  207.8 2.2 sum_pieces.1
  210.1 11.2 %convolution_convert_fusion = bf16[2048,768]{1,0:T(8,128)(2,1)} fusion(bf16[2048,2048]{1,0:T(8,128)(2,1)} %get-tuple-element.9, bf16[2048,768]{1,0:T(8,128)(2,1)} %bitcast.27), kind=kOutput, calls=%fused_computation.1 | convolution fusion | flops 6444023808 | bytes 14680064 | tf_op jit(solution)/shard_map/qp,pd->qd/dot_general | solution.py:167
  221.2 6.4 %all-gather.4.cloned.1.call-done = bf16[32,32,768]{2,1,0:T(8,128)(2,1)} async-done(((bf16[8,32,768]{2,1,0:T(8,128)(2,1)}), bf16[32,32,768]{2,1,0:T(8,128)(2,1)}) %all-gather.4.cloned.1.call-update) | async-done | bytes 1572880 | tf_op jit(solution)/shard_map/all_gather | solution.py:201
  227.6 1.8 convert_bitcast_fusion
  229.4 2.0 copy.27
  (25 shorter events, 1.0 us)
Async XLA Ops:
  25.1 1.4 copy-start
  29.2 5.9 %copy-start.3 = (s32[16,9]{1,0:T(8,128)S(1)}, s32[16,9]{1,0:T(8,128)}, u32[]{:S(2)}) copy-start(s32[16,9]{1,0:T(8,128)} %param.8) | copy-start | bytes 1732
  29.2 73.3 %all-to-all-start.1 = ((bf16[8,2,128,768]{3,2,1,0:T(8,128)(2,1)}), bf16[8,2,128,768]{3,2,1,0:T(8,128)(2,1)S(1)}, u32[]{:S(2)}, u32[]{:S(2)}) async-start(bf16[8,2,128,768]{3,2,1,0:T(8,128)(2,1)} %bitcast.5), calls=%async_computation.1 | async-start | bytes 6291456 | tf_op jit(solution)/shard_map/all_to_all | solution.py:184
  102.4 1.7 copy-start.1
  104.1 15.8 %copy-start.2 = (bf16[2048,768]{1,0:T(8,128)(2,1)S(1)}, bf16[2048,768]{1,0:T(8,128)(2,1)}, u32[]{:S(2)}) copy-start(bf16[2048,768]{1,0:T(8,128)(2,1)} %query_ref.1) | copy-start | bytes 9437188
  131.1 76.7 %all-to-all-start.2 = ((bf16[32,2,32,768]{3,2,1,0:T(8,128)(2,1)}), bf16[32,2,32,768]{3,2,1,0:T(8,128)(2,1)S(1)}, u32[]{:S(2)}, u32[]{:S(2)}) async-start(bf16[32,2,32,768]{3,2,1,0:T(8,128)(2,1)} %bitcast.28), calls=%async_computation.2 | async-start | bytes 6291456 | tf_op jit(solution)/shard_map/all_to_all | solution.py:192
  134.8 92.9 %all-gather.4.cloned.1.call-start = ((), (), s32[]{:S(2)}) async-start(), calls=%async_computation.3 | async-start | bytes 1966080 | tf_op jit(solution)/shard_map/all_gather | solution.py:201
Sparse Core Ops, SparseCore 0:
  210.2 17.3 all-gather.3
